TPU v7x, 32 devices: a whole 2x2x4 slice. The times are simulated.
32 devices in a mesh: runs: 2 (over x), gx: 16 (over z, y, core).
Axes of the slice: x: 2, y: 2, z: 4, core: 2. Of those that a mesh axis runs over, the one named last changes fastest.
Arguments:
- frac: float32 [3, 524288], P(None, ('runs', 'gx')), parts along dimension 1, may hold values from 0 to 1
- velocity: float32 [3, 524288], P(None, ('runs', 'gx')), parts along dimension 1, may hold values from -6 to 6
- mass: float32 [524288], P(('runs', 'gx')), parts along dimension 0, may hold values from 0.5 to 2
- particle_cell: int32 [524288], P(('runs', 'gx')), parts along dimension 0, may hold values from 0 to 8191, as said below
- tile_count: int32 [32], P(('runs', 'gx')), parts along dimension 0, may hold values from 2048 to 16384, as said below
- time_step: float32 [2], P('runs'), parts along dimension 0, may hold values from 0.1 to 0.2
Outputs:
- new_frac: float32 [3, 524288], P(None, ('runs', 'gx')), parts along dimension 1
- new_velocity: float32 [3, 524288], P(None, ('runs', 'gx')), parts along dimension 1
- next_step: float32 [2], P('runs'), parts along dimension 0
There are 2 independent parts, one for each index of `runs`. A program takes and returns all parts, laid end to end along the dimension named above; each array names one. Nothing has to cross between parts.
Inputs may be any that keep to these rules, and one draw needn't show every extreme that they name: `particle_cell`: within each tile the slots' cell numbers never fall; live slots come first and lie in cells with z <= 126; empty slots name the tile's last cell. `tile_count`: some tile is full in every run.
All inputs are finite; a program needn't handle non-finite values.
Results may differ from a plain program's by a relative error of at most 0.0003.
Values sent between devices are 32-bit elements; how exact they have to be, the bound alone decides.
No kernel may reach another device: no remote copies, remote signals or barrier semaphores. Data moves between devices by JAX's collectives and lax.ppermute only.
A program may use at most 64 MiB of HBM per device.

v0:
```python
import functools

import jax
import jax.numpy as jnp
from jax import lax
from jax.experimental import pallas as pl
from jax.experimental.pallas import tpu as pltpu
from jax.sharding import PartitionSpec as P

CX = 2
NY = 32
NZ = 128
ROWS = CX * NY
BLOCK = 256
LANES = 128
UNROLL = 8
FAST = 16
SPREAD = 32
TABLE = 16

mass_floor = 0.25
stiffness = 2.0
press_floor = 1.0
grain_size = 0.5
inertia_ref = 0.3
mu_static = 0.38
mu_limit = 0.64
rate_floor = 0.5
gravity = (0.5, 0.0, -0.866)
flip_share = 0.95
courant = 0.4
wave_speed = 2.0
components = ((0, 3, 4), (3, 1, 5), (4, 5, 2))
f32 = jnp.float32
bf16 = jnp.bfloat16


def split_pair(values):
    high = values.astype(bf16)
    low = (values - high.astype(f32)).astype(bf16)
    return high, low


def one_hot(cells_ref, block, offset):
    rel = cells_ref[pl.ds(block * 2, 2), :] - offset
    tall = (16, LANES)
    nodes = lax.broadcasted_iota(jnp.int32, tall, 0).astype(jnp.int16)
    one, zero = jnp.ones(tall, bf16), jnp.zeros(tall, bf16)
    halves = []
    for h in range(2):
        line = jnp.broadcast_to(rel[h : h + 1, :], tall).astype(jnp.int16)
        halves.append(
            jnp.concatenate(
                [
                    jnp.where(line == nodes + jnp.int16(z), one, zero)
                    for z in range(0, NZ, 16)
                ],
                axis=0,
            )
        )
    return jnp.concatenate(halves, axis=1)


def list_visits(cells_ref, count, plan_ref):
    blocks = cells_ref.shape[0] // 2
    shape = (blocks, LANES)
    number = lax.broadcasted_iota(jnp.int32, shape, 0)
    lane = lax.broadcasted_iota(jnp.int32, shape, 1)
    first_half = cells_ref[pl.ds(0, blocks, stride=2), :]
    second_half = cells_ref[pl.ds(1, blocks, stride=2), :]
    slot = number * BLOCK + lane
    reached = jnp.maximum(
        jnp.where(slot < count, first_half, 0), jnp.where(slot + LANES < count, second_half, 0)
    )
    live = number * BLOCK < count
    first = jnp.min(first_half, axis=1, keepdims=True) >> 7
    last = jnp.max(reached, axis=1, keepdims=True) >> 7
    low = jnp.where(live, first + number, 2 * LANES)
    high = jnp.where(live, last + number, -1)
    inside = (low <= lane) & (lane <= high)
    place = lane[:1]
    block = jnp.max(jnp.where(inside, number, -1), axis=0, keepdims=True)
    valid = block >= 0
    row = place - block
    plan_ref[0:1, :] = jnp.where(valid, block, 0)
    plan_ref[1:2, :] = jnp.where(valid, row + (row >> 5), 0)
    plan_ref[2:3, :] = jnp.where(valid, row, ROWS) * NZ
    plan_ref[3:4, :] = jnp.max(high, axis=0, keepdims=True) + 1
    plan_ref[4:5, :] = jnp.broadcast_to(count, (1, LANES))
    plan_ref[5:8, :] = jnp.zeros((3, LANES), jnp.int32)


def spread_kernel(
    count_ref, frac_hbm, vel_hbm, mass_hbm, cells_hbm,
    far_ref, near_ref, plan_ref, frac_ref, vel_ref, cells_ref,
    listed_ref, mass_ref, q_ref, acc_ref, sems,
):
    slots = frac_ref.shape[1]
    sources = (cells_hbm, frac_hbm, vel_hbm, mass_hbm)
    targets = (cells_ref, frac_ref, vel_ref, mass_ref)
    arrivals = [
        pltpu.make_async_copy(source, target, sems.at[k])
        for k, (source, target) in enumerate(zip(sources, targets))
    ]
    for arrival in arrivals:
        arrival.start()
    acc_ref[...] = jnp.zeros_like(acc_ref)
    arrivals[0].wait()
    count = count_ref[0]
    list_visits(cells_ref, count, plan_ref)
    listing = pltpu.make_async_copy(plan_ref, listed_ref, sems.at[4])
    listing.start()
    for arrival in arrivals[1:]:
        arrival.wait()
    sublane = lax.broadcasted_iota(jnp.int32, (8, LANES), 0)
    lane = lax.broadcasted_iota(jnp.int32, (1, LANES), 1)
    top_z = sublane >= 4
    field = sublane & 3

    def weigh(part):
        at = pl.multiple_of(part * LANES, LANES)
        here = pl.ds(at, LANES)

        def spread_out(line):
            return jnp.broadcast_to(line, (8, LANES))

        fx, fy, fz = (spread_out(frac_ref[d : d + 1, here]) for d in range(3))
        vx, vy, vz = (spread_out(vel_ref[d : d + 1, here]) for d in range(3))
        held = spread_out(jnp.where(at + lane < count, mass_ref[pl.ds(part, 1), :], 0.0))
        carried = jnp.where(
            field == 0, held, held * jnp.where(field == 1, vx, jnp.where(field == 2, vy, vz))
        )
        carried = carried * jnp.where(top_z, fz, 1.0 - fz)
        lower, upper = carried * (1.0 - fx), carried * fx
        rows = jnp.concatenate(
            [lower * (1.0 - fy), lower * fy, upper * (1.0 - fy), upper * fy], axis=0
        )
        high, low = split_pair(rows)
        q_ref[pl.ds(part, 1)] = jnp.concatenate([high, low], axis=0)[None]

    def prepare(group, carry):
        for u in range(UNROLL):
            weigh(group * UNROLL + u)
        return carry

    lax.fori_loop(0, slots // LANES // UNROLL, prepare, 0)
    listing.wait()
    total = listed_ref[3, 0]

    def visit(group, carry):
        found = []
        for u in range(FAST):
            v = group * FAST + u
            block = listed_ref[0, v]
            hot = one_hot(cells_ref, block, listed_ref[2, v])
            both = q_ref[pl.ds(block * 2, 2)]
            both = lax.dot_general(
                jnp.concatenate([both[0], both[1]], axis=1),
                hot,
                (((1,), (1,)), ((), ())),
                preferred_element_type=f32,
            )
            found.append((listed_ref[1, v], both[:SPREAD] + both[SPREAD:]))
        for base, part in found:
            for k, ahead in enumerate((0, 1, NY + 1, NY + 2)):
                at = pl.ds(pl.multiple_of((base + ahead) * 8, 8), 8)
                acc_ref[at, :] += part[8 * k : 8 * k + 8]
        return carry

    lax.fori_loop(0, (total + FAST - 1) // FAST, visit, 0)

    layers = []
    for l in range(CX + 1):
        first = l * (NY + 1) * 8
        acc_ref[first : first + 8, :] += acc_ref[first + NY * 8 : first + NY * 8 + 8, :]
        for f in range(4):
            lower = acc_ref[pl.ds(first + f, NY, stride=8), :]
            upper = acc_ref[pl.ds(first + 4 + f, NY, stride=8), :]
            layers.append(lower + pltpu.roll(upper, 1, 1))
    odd = lax.axis_index("gx") % 2 == 1
    for l in range(CX):
        for f in range(4):
            low, high = layers[l * 4 + f], layers[(l + 1) * 4 + f]
            near_ref[f * CX + l] = jnp.where(odd, low, high)
            far_ref[f * CX + l] = jnp.where(odd, high, low)


def pair_up(field, axis):
    return field + pltpu.roll(field, field.shape[axis] - 1, axis)


def step_up(field, axis):
    return pltpu.roll(field, field.shape[axis] - 1, axis) - field


def pair_down(field, axis):
    return field + pltpu.roll(field, 1, axis)


def step_down(field, axis):
    return field - pltpu.roll(field, 1, axis)


def cell_stress(vel_lo, vel_hi, mass_lo, mass_hi, keep):
    grads = []
    for a in range(3):
        diff = vel_hi[a] - vel_lo[a]
        both = vel_hi[a] + vel_lo[a]
        grads.append(
            [
                0.25 * pair_up(pair_up(diff, 0), 1),
                0.25 * pair_up(step_up(both, 0), 1),
                0.25 * step_up(pair_up(both, 0), 1),
            ]
        )
    density = 0.125 * pair_up(pair_up(mass_hi + mass_lo, 0), 1)
    dxx = grads[0][0]
    dyy = grads[1][1]
    dzz = grads[2][2]
    dxy = 0.5 * (grads[0][1] + grads[1][0])
    dxz = 0.5 * (grads[0][2] + grads[2][0])
    dyz = 0.5 * (grads[1][2] + grads[2][1])
    second = dxx * dxx + dyy * dyy + dzz * dzz + 2.0 * (dxy * dxy + dxz * dxz + dyz * dyz)
    rate = jnp.sqrt(2.0 * second + rate_floor * rate_floor)
    pressure = stiffness * density
    inertial = rate * grain_size / jnp.sqrt(pressure + press_floor)
    friction = mu_static + (mu_limit - mu_static) * inertial / (inertia_ref + inertial)
    twice = 2.0 * friction * pressure / rate
    sigma = [
        twice * dxx - pressure,
        twice * dyy - pressure,
        twice * dzz - pressure,
        twice * dxy,
        twice * dxz,
        twice * dyz,
    ]
    return [jnp.where(keep, s, 0.0) for s in sigma]


def node_force(lower, upper):
    force = []
    for a in range(3):
        sx, sy, sz = (components[a][b] for b in range(3))
        along = pair_down(pair_down(upper[sx] - lower[sx], 0), 1)
        across = step_down(pair_down(upper[sy] + lower[sy], 1), 0)
        upward = step_down(pair_down(upper[sz] + lower[sz], 0), 1)
        force.append(0.25 * (along + across + upward))
    return force


def collect_kernel(
    step_ref, plan_ref, near_ref, far_ref, far_new_ref, near_new_ref, frac_ref, vel_ref, cells_ref,
    out_ref, top_ref, listed_ref, tab_ref, pair_ref, sem,
):
    blocks = frac_ref.shape[1] // BLOCK
    listing = pltpu.make_async_copy(plan_ref, listed_ref, sem)
    listing.start()
    step = step_ref[0]
    odd = lax.axis_index("gx") % 2 == 1

    def pick(if_odd, if_even):
        return [jnp.where(odd, if_odd[k], if_even[k]) for k in range(4 * CX)]

    low, high = pick(near_ref, far_ref), pick(far_ref, near_ref)
    left, right = pick(near_new_ref, far_new_ref), pick(far_new_ref, near_new_ref)
    nodes = [
        [left[f * 2] for f in range(4)],
        [low[f * 2] + left[f * 2 + 1] for f in range(4)],
        [low[f * 2 + 1] for f in range(4)],
        [high[f * 2 + 1] + right[f * 2] for f in range(4)],
        [right[f * 2 + 1] for f in range(4)],
    ]
    height = lax.broadcasted_iota(jnp.int32, (NY, NZ), 1)
    keep = height < NZ - 1
    above_bed = height > 0
    floor = [jnp.maximum(layer[0], mass_floor) for layer in nodes]
    v_old = [[layer[1 + a] / floor[l] for a in range(3)] for l, layer in enumerate(nodes)]
    sigma = [
        cell_stress(v_old[l], v_old[l + 1], nodes[l][0], nodes[l + 1][0], keep) for l in range(4)
    ]
    blank = jnp.zeros((NY, NZ), f32)
    for l in range(CX + 1):
        force = node_force(sigma[l], sigma[l + 1])
        fields = [blank] * 8
        for a in range(3):
            layer = nodes[l + 1]
            fresh = (layer[1 + a] + step * (force[a] + layer[0] * gravity[a])) / floor[l + 1]
            fresh = jnp.where(above_bed, fresh, 0.0)
            fields[a] = fresh - flip_share * v_old[l + 1][a]
            fields[4 + a] = step * fresh
        for k, value in enumerate(fields):
            start = l * NY * TABLE + k
            tab_ref[pl.ds(start, NY, stride=TABLE), :] = value
            tab_ref[pl.ds(start + 8, NY, stride=TABLE), :] = pltpu.roll(value, NZ - 1, 1)

    for l in range(CX + 1):

        def split_row(j, carry):
            at = pl.ds(pl.multiple_of((l * NY + j) * TABLE, TABLE), TABLE)
            high, low = split_pair(tab_ref[at, :])
            pair_ref[pl.ds(l * (NY + 1) + j, 1)] = jnp.concatenate([high, low], axis=1)[None]
            return carry

        lax.fori_loop(0, NY, split_row, 0, unroll=8)
        pair_ref[l * (NY + 1) + NY] = pair_ref[l * (NY + 1)]

    out_ref[...] = jnp.zeros_like(out_ref)
    listing.wait()
    total = listed_ref[3, 0]
    count = listed_ref[4, 0]

    def visit(group, carry):
        found = []
        for u in range(UNROLL):
            v = group * UNROLL + u
            block = listed_ref[0, v]
            base = listed_ref[1, v]
            hot = one_hot(cells_ref, block, listed_ref[2, v])
            rows = [pair_ref[base + ahead] for ahead in (0, 1, NY + 1, NY + 2)]
            value = jnp.dot(
                jnp.concatenate(rows, axis=0),
                jnp.concatenate([hot, hot], axis=0),
                preferred_element_type=f32,
            )
            corners = [value[8 * k : 8 * k + 8] for k in range(8)]
            frac = frac_ref[:, pl.ds(pl.multiple_of(block * BLOCK, BLOCK), BLOCK)]
            for d in (2, 1, 0):
                share = frac[d : d + 1, :]
                corners = [
                    corners[k] + share * (corners[k + 1] - corners[k])
                    for k in range(0, len(corners), 2)
                ]
            found.append((block, corners[0]))
        for block, part in found:
            out_ref[pl.ds(block, 1)] += part[None]
        return carry

    lax.fori_loop(0, (total + UNROLL - 1) // UNROLL, visit, 0)

    lane = lax.broadcasted_iota(jnp.int32, (1, BLOCK), 1)

    def finish(block, top):
        at = pl.multiple_of(block * BLOCK, BLOCK)
        alive = at + lane < count
        got = out_ref[pl.ds(block, 1)][0]
        fresh = jnp.where(alive, flip_share * vel_ref[:, pl.ds(at, BLOCK)] + got[0:3], 0.0)
        out_ref[pl.ds(block, 1), 0:3] = fresh[None]
        square = fresh[0:1] * fresh[0:1] + fresh[1:2] * fresh[1:2] + fresh[2:3] * fresh[2:3]
        return jnp.maximum(top, square)

    top = lax.fori_loop(0, blocks, finish, jnp.zeros((1, BLOCK), f32), unroll=4)
    top = jnp.sqrt(jnp.max(top, axis=1, keepdims=True))
    top_ref[...] = jnp.broadcast_to(top, top_ref.shape)


def finish_kernel(plan_ref, moved_ref, frac_ref, new_frac_ref, new_vel_ref):
    blocks = frac_ref.shape[1] // BLOCK
    count = plan_ref[4:5, :]
    count = jnp.concatenate([count, count], axis=1)
    lane = lax.broadcasted_iota(jnp.int32, (1, BLOCK), 1)

    def finish(block, carry):
        at = pl.multiple_of(block * BLOCK, BLOCK)
        got = moved_ref[pl.ds(block, 1)][0]
        new_vel_ref[:, pl.ds(at, BLOCK)] = got[0:3]
        placed = jnp.where(at + lane < count, frac_ref[:, pl.ds(at, BLOCK)] + got[4:7], 0.0)
        new_frac_ref[:, pl.ds(at, BLOCK)] = placed
        return carry

    lax.fori_loop(0, blocks, finish, 0, unroll=4)


def largest(value, axis):
    devices = lax.axis_size(axis)
    reach = 1
    while reach < devices:
        if devices & (devices - 1) == 0:
            pairs = [(i, i ^ (reach | 1)) for i in range(devices)]
        else:
            pairs = [(i, (i + reach) % devices) for i in range(devices)]
        value = jnp.maximum(value, lax.ppermute(value, axis, pairs))
        reach *= 2
    return value


smem = pl.BlockSpec(memory_space=pltpu.SMEM)
vmem = pl.BlockSpec(memory_space=pltpu.VMEM)
hbm = pl.BlockSpec(memory_space=pltpu.HBM)


def body(frac, velocity, mass, particle_cell, tile_count, time_step):
    slots = frac.shape[1]
    blocks = slots // BLOCK
    rows = slots // LANES
    inputs = (frac, velocity, mass.reshape(rows, LANES), particle_cell.reshape(rows, LANES))
    layer_pair = pltpu.VMEM((4 * CX, NY, NZ), f32)
    far, near, plan, frac_here, vel_here, cells_here = pl.pallas_call(
        spread_kernel,
        out_shape=(
            layer_pair,
            layer_pair,
            pltpu.VMEM((8, LANES), jnp.int32),
            pltpu.VMEM(frac.shape, f32),
            pltpu.VMEM(velocity.shape, f32),
            pltpu.VMEM((rows, LANES), jnp.int32),
        ),
        in_specs=[smem] + [hbm] * 4,
        out_specs=(vmem,) * 6,
        scratch_shapes=[
            pltpu.SMEM((8, LANES), jnp.int32),
            pltpu.VMEM((rows, LANES), f32),
            pltpu.VMEM((rows, 2 * SPREAD, LANES), bf16),
            pltpu.VMEM(((CX + 1) * (NY + 1) * 8, NZ), f32),
            pltpu.SemaphoreType.DMA((5,)),
        ],
        compiler_params=pltpu.CompilerParams(vmem_limit_bytes=32 * 1024 * 1024),
        name="spread",
    )(tile_count, *[pltpu.with_memory_space_constraint(x, pltpu.HBM) for x in inputs])
    devices = lax.axis_size("gx")
    far_pairs = [(i, (i + (1 if i % 2 else -1)) % devices) for i in range(devices)]
    near_pairs = [(i, i ^ 1) for i in range(devices)]
    near_new = lax.ppermute(near, "gx", near_pairs)
    far_new = lax.ppermute(far, "gx", far_pairs)
    moved, top = pl.pallas_call(
        collect_kernel,
        out_shape=(
            jax.ShapeDtypeStruct((blocks, 8, BLOCK), f32),
            jax.ShapeDtypeStruct((8, LANES), f32),
        ),
        in_specs=[smem] + [vmem] * 8,
        out_specs=(vmem, vmem),
        scratch_shapes=[
            pltpu.SMEM((8, LANES), jnp.int32),
            pltpu.VMEM(((CX + 1) * NY * TABLE, NZ), f32),
            pltpu.VMEM(((CX + 1) * (NY + 1), TABLE, 2 * NZ), bf16),
            pltpu.SemaphoreType.DMA,
        ],
        compiler_params=pltpu.CompilerParams(vmem_limit_bytes=32 * 1024 * 1024),
        name="collect",
    )(time_step, plan, near, far, far_new, near_new, frac_here, vel_here, cells_here)
    new_frac, new_velocity = pl.pallas_call(
        finish_kernel,
        out_shape=(
            jax.ShapeDtypeStruct(frac.shape, f32),
            jax.ShapeDtypeStruct(velocity.shape, f32),
        ),
        in_specs=[vmem] * 3,
        out_specs=(vmem, vmem),
        compiler_params=pltpu.CompilerParams(vmem_limit_bytes=32 * 1024 * 1024),
        cost_estimate=pl.CostEstimate(flops=0, bytes_accessed=8000000, transcendentals=0),
        name="finish",
    )(plan, moved, frac_here)
    fastest = largest(top, "gx")
    next_step = (courant / (fastest + wave_speed))[0, :1]
    return (new_frac, new_velocity, next_step)


def solution(mesh):
    placed = (
        P(None, ("runs", "gx")),
        P(None, ("runs", "gx")),
        P(("runs", "gx")),
        P(("runs", "gx")),
        P(("runs", "gx")),
        P("runs"),
    )
    return jax.shard_map(
        body,
        mesh=mesh,
        in_specs=placed,
        out_specs=(P(None, ("runs", "gx")), P(None, ("runs", "gx")), P("runs")),
        check_vma=False,
    )
```

profile of v0, /device:TPU:0, one launch (start us, length us, event | category | flops | bytes accessed | tf_op | source)
XLA Modules:
  0.0 34.6 jit_solution(6245508031055417975)
XLA Ops:
  1.3 6.0 %spread.1 = (f32[8,32,128]{2,1,0:T(8,128)S(1)}, f32[8,32,128]{2,1,0:T(8,128)S(1)}, s32[8,128]{1,0:T(8,128)S(1)}, f32[3,16384]{1,0:T(4,128)S(1)}, f32[3,16384]{1,0:T(4,128)S(1)}, /*index=5*/s32[128,128]{1,0:T(8,128)S(1)}) custom-call(s32[1]{0:T(128)S(6)} %copy.9.count_ref, f32[3,16384]{1,0:T(4,128)} %frac_hbm.1, f32[3,16384]{1,0:T(4,128)} %vel_hbm.1, ...), custom_call_target="tpu_custom_call" | custom-call | tf_op jit(solution)/shard_map/spread/pallas_call | solution.py:397
  7.3 0.1 collective-permute-start.1
  7.4 6.1 %collective-permute-start = (f32[8,32,128]{2,1,0:T(8,128)S(1)}, f32[8,32,128]{2,1,0:T(8,128)S(1)}, u32[]{:S(2)}, u32[]{:S(2)}) collective-permute-start(f32[8,32,128]{2,1,0:T(8,128)S(1)} %get-tuple-element.15.far_ref), channel_id=1, source_target_pairs={{0,15},{1,2},{2,1},{3,4},{4,3},{5,6},{6,5},{7,8},{8,7},{9,10},{10,... | collective-permute-start | bytes 393224 | tf_op jit(solution)/shard_map/ppermute | solution.py:423
  14.1 0.0 collective-permute-done.1.near_new_ref
  14.2 2.0 %collective-permute-done.far_new_ref = f32[8,32,128]{2,1,0:T(8,128)S(1)} collective-permute-done((f32[8,32,128]{2,1,0:T(8,128)S(1)}, f32[8,32,128]{2,1,0:T(8,128)S(1)}, u32[]{:S(2)}, u32[]{:S(2)}) %collective-permute-start) | collective-permute-done | bytes 131104 | tf_op jit(solution)/shard_map/ppermute | solution.py:423
  16.1 6.6 %collect.1 = (f32[64,8,256]{2,1,0:T(8,128)S(1)}, f32[8,128]{1,0:T(8,128)S(1)}) custom-call(f32[1]{0:T(128)S(6)} %copy.10.step_ref, s32[8,128]{1,0:T(8,128)S(1)} %get-tuple-element.13.plan_ref, f32[8,32,128]{2,1,0:T(8,128)S(1)} %get-tuple-element.14.near_ref, f32[8,32,128]{2,1,0:T(8,128)S(1)} %get-tuple-element.15.far_ref, ...), custom_call_target="tpu_custom_call" | custom-call | tf_op jit(solution)/shard_map/collect/pallas_call | solution.py:424
  22.8 0.1 collective-permute-start.2
  22.9 1.2 %collective-permute-done.2 = f32[8,128]{1,0:T(8,128)S(1)} collective-permute-done((f32[8,128]{1,0:T(8,128)S(1)}, f32[8,128]{1,0:T(8,128)S(1)}, u32[]{:S(2)}, u32[]{:S(2)}) %collective-permute-start.2) | collective-permute-done | bytes 4128 | tf_op jit(solution)/shard_map/ppermute | solution.py:381
  24.0 0.0 collective-permute-start.3
  24.0 3.0 %collective-permute-done.3 = f32[8,128]{1,0:T(8,128)S(1)} collective-permute-done((f32[8,128]{1,0:T(8,128)S(1)}, f32[8,128]{1,0:T(8,128)S(1)}, u32[]{:S(2)}, u32[]{:S(2)}) %collective-permute-start.3) | collective-permute-done | bytes 4128 | tf_op jit(solution)/shard_map/ppermute | solution.py:381
  27.0 0.0 collective-permute-start.4
  27.1 3.0 %collective-permute-done.4 = f32[8,128]{1,0:T(8,128)S(1)} collective-permute-done((f32[8,128]{1,0:T(8,128)S(1)}, f32[8,128]{1,0:T(8,128)S(1)}, u32[]{:S(2)}, u32[]{:S(2)}) %collective-permute-start.4) | collective-permute-done | bytes 4128 | tf_op jit(solution)/shard_map/ppermute | solution.py:381
  30.1 0.8 %collective-permute-start.5 = (f32[8,128]{1,0:T(8,128)S(1)}, f32[8,128]{1,0:T(8,128)S(1)}, u32[]{:S(2)}, u32[]{:S(2)}) collective-permute-start(f32[8,128]{1,0:T(8,128)S(1)} %max.14), channel_id=1, source_target_pairs={{0,9},{1,8},{2,11},{3,10},{4,13},{5,12},{6,15},{7,14},{8,1},{9,0},... | collective-permute-start | bytes 12296 | tf_op jit(solution)/shard_map/ppermute | solution.py:381
  30.9 1.0 %finish.1 = (f32[3,16384]{1,0:T(4,128)}, f32[3,16384]{1,0:T(4,128)}) custom-call(s32[8,128]{1,0:T(8,128)S(1)} %get-tuple-element.13.plan_ref, f32[64,8,256]{2,1,0:T(8,128)S(1)} %get-tuple-element.19.moved_ref, f32[3,16384]{1,0:T(4,128)S(1)} %get-tuple-element.16.frac_ref), custom_call_target="tpu_custom_call" | custom-call | bytes 8000000 | tf_op jit(solution)/shard_map/finish/pallas_call | solution.py:441
  31.9 2.1 %collective-permute-done.5 = f32[8,128]{1,0:T(8,128)S(1)} collective-permute-done((f32[8,128]{1,0:T(8,128)S(1)}, f32[8,128]{1,0:T(8,128)S(1)}, u32[]{:S(2)}, u32[]{:S(2)}) %collective-permute-start.5) | collective-permute-done | bytes 4128 | tf_op jit(solution)/shard_map/ppermute | solution.py:381
  34.0 0.5 %slice.3 = f32[1,1]{1,0:T(1,128)} slice(f32[8,128]{1,0:T(8,128)S(1)} %add_divide_fusion), slice={[0:1], [0:1]} | slice | bytes 8 | tf_op jit(solution)/shard_map/slice | solution.py:454
  (4 shorter events, 0.0 us)
Async XLA Ops:
  7.3 6.8 %collective-permute-start.1 = (f32[8,32,128]{2,1,0:T(8,128)S(1)}, f32[8,32,128]{2,1,0:T(8,128)S(1)}, u32[]{:S(2)}, u32[]{:S(2)}) collective-permute-start(f32[8,32,128]{2,1,0:T(8,128)S(1)} %get-tuple-element.14.near_ref), channel_id=1, source_target_pairs={{0,1},{1,0},{2,3},{3,2},{4,5},{5,4},{6,7},{7,6},{8,9},{9,8},{10,11... | collective-permute-start | bytes 393224 | tf_op jit(solution)/shard_map/ppermute | solution.py:422
  7.4 8.7 %collective-permute-start = (f32[8,32,128]{2,1,0:T(8,128)S(1)}, f32[8,32,128]{2,1,0:T(8,128)S(1)}, u32[]{:S(2)}, u32[]{:S(2)}) collective-permute-start(f32[8,32,128]{2,1,0:T(8,128)S(1)} %get-tuple-element.15.far_ref), channel_id=1, source_target_pairs={{0,15},{1,2},{2,1},{3,4},{4,3},{5,6},{6,5},{7,8},{8,7},{9,10},{10,... | collective-permute-start | bytes 393224 | tf_op jit(solution)/shard_map/ppermute | solution.py:423
  22.8 1.2 %collective-permute-start.2 = (f32[8,128]{1,0:T(8,128)S(1)}, f32[8,128]{1,0:T(8,128)S(1)}, u32[]{:S(2)}, u32[]{:S(2)}) collective-permute-start(f32[8,128]{1,0:T(8,128)S(1)} %get-tuple-element.22), channel_id=1, source_target_pairs={{0,1},{1,0},{2,3},{3,2},{4,5},{5,4},{6,7},{7,6},{8,9},{9,8},{10,11... | collective-permute-start | bytes 12296 | tf_op jit(solution)/shard_map/ppermute | solution.py:381
  24.0 3.0 %collective-permute-start.3 = (f32[8,128]{1,0:T(8,128)S(1)}, f32[8,128]{1,0:T(8,128)S(1)}, u32[]{:S(2)}, u32[]{:S(2)}) collective-permute-start(f32[8,128]{1,0:T(8,128)S(1)} %max.12), channel_id=1, source_target_pairs={{0,3},{1,2},{2,1},{3,0},{4,7},{5,6},{6,5},{7,4},{8,11},{9,10},{10,... | collective-permute-start | bytes 12296 | tf_op jit(solution)/shard_map/ppermute | solution.py:381
  27.0 3.0 %collective-permute-start.4 = (f32[8,128]{1,0:T(8,128)S(1)}, f32[8,128]{1,0:T(8,128)S(1)}, u32[]{:S(2)}, u32[]{:S(2)}) collective-permute-start(f32[8,128]{1,0:T(8,128)S(1)} %max.13), channel_id=1, source_target_pairs={{0,5},{1,4},{2,7},{3,6},{4,1},{5,0},{6,3},{7,2},{8,13},{9,12},{10,... | collective-permute-start | bytes 12296 | tf_op jit(solution)/shard_map/ppermute | solution.py:381
  30.1 3.9 %collective-permute-start.5 = (f32[8,128]{1,0:T(8,128)S(1)}, f32[8,128]{1,0:T(8,128)S(1)}, u32[]{:S(2)}, u32[]{:S(2)}) collective-permute-start(f32[8,128]{1,0:T(8,128)S(1)} %max.14), channel_id=1, source_target_pairs={{0,9},{1,8},{2,11},{3,10},{4,13},{5,12},{6,15},{7,14},{8,1},{9,0},... | collective-permute-start | bytes 12296 | tf_op jit(solution)/shard_map/ppermute | solution.py:381
where the time goes:
time: 33.9 us; the launch traced here: 34.6 us
  Pallas kernels  13.7 us (40%)
  waiting for transfers between devices  11.3 us (33%)
  starting transfers between devices  7.04 us (21%)
  between operations  1.98 us (6%)
  local copies, waits for them, and re-layouts  0.52 us (2%)
    ppermute x4, waiting for transfers between devices, largest(): value = jnp.maximum(value, lax.ppermute(value, axis, pairs))  9.35 us
    pallas_call x1, Pallas kernels, body(): pl.pallas_call(collect_kernel, out_shape=(jax.ShapeDtypeStruct((blocks, 8...  6.63 us
    ppermute x1, starting transfers between devices, body(): far_new = lax.ppermute(far, 'gx', far_pairs)  6.09 us
    pallas_call x1, Pallas kernels, body(): pl.pallas_call(spread_kernel, out_shape=(layer_pair, layer_pair, pltpu.VM...  6.03 us
    ppermute x1, waiting for transfers between devices, body(): far_new = lax.ppermute(far, 'gx', far_pairs)  1.99 us
    pallas_call x1, Pallas kernels, body(): pl.pallas_call(finish_kernel, out_shape=(jax.ShapeDtypeStruct(frac.shape,...  1 us
    ppermute x4, starting transfers between devices, largest(): value = jnp.maximum(value, lax.ppermute(value, axis, pairs))  0.88 us
  transfers between devices with their start and end apart: 6, of which 5 were waited for; matrix products, arithmetic and copies ran while one was open for 0% of the time, Pallas kernels for 3%

commit v1 on v0

--- a/solution.py
+++ b/solution.py
@@ -14,7 +14,8 @@
 BLOCK = 256
 LANES = 128
 UNROLL = 8
-FAST = 16
+GIVEN = 32
+TAKEN = 16
 SPREAD = 32
 TABLE = 16
 
@@ -149,8 +150,8 @@
 
     def visit(group, carry):
         found = []
-        for u in range(FAST):
-            v = group * FAST + u
+        for u in range(GIVEN):
+            v = group * GIVEN + u
             block = listed_ref[0, v]
             hot = one_hot(cells_ref, block, listed_ref[2, v])
             both = q_ref[pl.ds(block * 2, 2)]
@@ -167,7 +168,7 @@
                 acc_ref[at, :] += part[8 * k : 8 * k + 8]
         return carry
 
-    lax.fori_loop(0, (total + FAST - 1) // FAST, visit, 0)
+    lax.fori_loop(0, (total + GIVEN - 1) // GIVEN, visit, 0)
 
     layers = []
     for l in range(CX + 1):
@@ -311,8 +312,8 @@
 
     def visit(group, carry):
         found = []
-        for u in range(UNROLL):
-            v = group * UNROLL + u
+        for u in range(TAKEN):
+            v = group * TAKEN + u
             block = listed_ref[0, v]
             base = listed_ref[1, v]
             hot = one_hot(cells_ref, block, listed_ref[2, v])
@@ -335,7 +336,7 @@
             out_ref[pl.ds(block, 1)] += part[None]
         return carry
 
-    lax.fori_loop(0, (total + UNROLL - 1) // UNROLL, visit, 0)
+    lax.fori_loop(0, (total + TAKEN - 1) // TAKEN, visit, 0)
 
     lane = lax.broadcasted_iota(jnp.int32, (1, BLOCK), 1)
 

time: 33.9 us -> 31.9 us (0.941); the launches traced: 34.6 us -> 31.5 us
  Pallas kernels: 13.7 us -> 9.71 us
  starting transfers between devices: 7.04 us -> 10.6 us
  waiting for transfers between devices: 11.3 us -> 8.66 us
    ppermute x4, waiting for transfers between devices: 9.35 us -> 6.67 us  [largest(): value = jnp.maximum(value, lax.ppermute(value, axis, pairs))]
    ppermute x4, starting transfers between devices: 0.88 us -> 3.55 us  [largest(): value = jnp.maximum(value, lax.ppermute(value, axis, pairs))]
    pallas_call x1, Pallas kernels: 6.63 us -> 4.05 us  [body(): pl.pallas_call(collect_kernel, out_shape=(jax.ShapeDtypeStruct((blocks, 8...]
    pallas_call x1, Pallas kernels: 6.03 us -> 4.66 us  [body(): pl.pallas_call(spread_kernel, out_shape=(layer_pair, layer_pair, pltpu.VM...]
    ppermute x1, starting transfers between devices: 6.09 us -> 6.56 us  [body(): far_new = lax.ppermute(far, 'gx', far_pairs)]
    ppermute x1, starting transfers between devices: 0.07 us -> 0.53 us  [body(): near_new = lax.ppermute(near, 'gx', near_pairs)]
where the time goes in v1:
time: 31.9 us; the launch traced here: 31.5 us
  starting transfers between devices  10.6 us (33%)
  Pallas kernels  9.71 us (30%)
  waiting for transfers between devices  8.66 us (27%)
  between operations  1.97 us (6%)
  local copies, waits for them, and re-layouts  0.52 us (2%)
    ppermute x4, waiting for transfers between devices, largest(): value = jnp.maximum(value, lax.ppermute(value, axis, pairs))  6.67 us
    ppermute x1, starting transfers between devices, body(): far_new = lax.ppermute(far, 'gx', far_pairs)  6.56 us
    pallas_call x1, Pallas kernels, body(): pl.pallas_call(spread_kernel, out_shape=(layer_pair, layer_pair, pltpu.VM...  4.66 us
    pallas_call x1, Pallas kernels, body(): pl.pallas_call(collect_kernel, out_shape=(jax.ShapeDtypeStruct((blocks, 8...  4.05 us
    ppermute x4, starting transfers between devices, largest(): value = jnp.maximum(value, lax.ppermute(value, axis, pairs))  3.55 us
    ppermute x1, waiting for transfers between devices, body(): far_new = lax.ppermute(far, 'gx', far_pairs)  1.99 us
    pallas_call x1, Pallas kernels, body(): pl.pallas_call(finish_kernel, out_shape=(jax.ShapeDtypeStruct(frac.shape,...  1 us
  transfers between devices with their start and end apart: 6, of which 5 were waited for; matrix products, arithmetic and copies ran while one was open for 0% of the time, Pallas kernels for 3%

profile of v1, /device:TPU:0, one launch (start us, length us, event | category | flops | bytes accessed | tf_op | source)
XLA Modules:
  0.0 31.5 jit_solution(14539459304501725232)
XLA Ops:
  1.3 4.7 %spread.1 = (f32[8,32,128]{2,1,0:T(8,128)S(1)}, f32[8,32,128]{2,1,0:T(8,128)S(1)}, s32[8,128]{1,0:T(8,128)S(1)}, f32[3,16384]{1,0:T(4,128)S(1)}, f32[3,16384]{1,0:T(4,128)S(1)}, /*index=5*/s32[128,128]{1,0:T(8,128)S(1)}) custom-call(s32[1]{0:T(128)S(6)} %copy.9.count_ref, f32[3,16384]{1,0:T(4,128)} %frac_hbm.1, f32[3,16384]{1,0:T(4,128)} %vel_hbm.1, ...), custom_call_target="tpu_custom_call" | custom-call | tf_op jit(solution)/shard_map/spread/pallas_call | solution.py:398
  5.9 0.5 %collective-permute-start.1 = (f32[8,32,128]{2,1,0:T(8,128)S(1)}, f32[8,32,128]{2,1,0:T(8,128)S(1)}, u32[]{:S(2)}, u32[]{:S(2)}) collective-permute-start(f32[8,32,128]{2,1,0:T(8,128)S(1)} %get-tuple-element.14.near_ref), channel_id=1, source_target_pairs={{0,1},{1,0},{2,3},{3,2},{4,5},{5,4},{6,7},{7,6},{8,9},{9,8},{10,11... | collective-permute-start | bytes 393224 | tf_op jit(solution)/shard_map/ppermute | solution.py:423
  6.5 6.6 %collective-permute-start = (f32[8,32,128]{2,1,0:T(8,128)S(1)}, f32[8,32,128]{2,1,0:T(8,128)S(1)}, u32[]{:S(2)}, u32[]{:S(2)}) collective-permute-start(f32[8,32,128]{2,1,0:T(8,128)S(1)} %get-tuple-element.15.far_ref), channel_id=1, source_target_pairs={{0,15},{1,2},{2,1},{3,4},{4,3},{5,6},{6,5},{7,8},{8,7},{9,10},{10,... | collective-permute-start | bytes 393224 | tf_op jit(solution)/shard_map/ppermute | solution.py:424
  13.7 0.0 collective-permute-done.1.near_new_ref
  13.7 2.0 %collective-permute-done.far_new_ref = f32[8,32,128]{2,1,0:T(8,128)S(1)} collective-permute-done((f32[8,32,128]{2,1,0:T(8,128)S(1)}, f32[8,32,128]{2,1,0:T(8,128)S(1)}, u32[]{:S(2)}, u32[]{:S(2)}) %collective-permute-start) | collective-permute-done | bytes 131104 | tf_op jit(solution)/shard_map/ppermute | solution.py:424
  15.7 4.0 %collect.1 = (f32[64,8,256]{2,1,0:T(8,128)S(1)}, f32[8,128]{1,0:T(8,128)S(1)}) custom-call(f32[1]{0:T(128)S(6)} %copy.10.step_ref, s32[8,128]{1,0:T(8,128)S(1)} %get-tuple-element.13.plan_ref, f32[8,32,128]{2,1,0:T(8,128)S(1)} %get-tuple-element.14.near_ref, f32[8,32,128]{2,1,0:T(8,128)S(1)} %get-tuple-element.15.far_ref, ...), custom_call_target="tpu_custom_call" | custom-call | tf_op jit(solution)/shard_map/collect/pallas_call | solution.py:425
  19.7 0.1 collective-permute-start.2
  19.8 1.2 %collective-permute-done.2 = f32[8,128]{1,0:T(8,128)S(1)} collective-permute-done((f32[8,128]{1,0:T(8,128)S(1)}, f32[8,128]{1,0:T(8,128)S(1)}, u32[]{:S(2)}, u32[]{:S(2)}) %collective-permute-start.2) | collective-permute-done | bytes 4128 | tf_op jit(solution)/shard_map/ppermute | solution.py:382
  21.0 0.6 %collective-permute-start.3 = (f32[8,128]{1,0:T(8,128)S(1)}, f32[8,128]{1,0:T(8,128)S(1)}, u32[]{:S(2)}, u32[]{:S(2)}) collective-permute-start(f32[8,128]{1,0:T(8,128)S(1)} %max.12), channel_id=1, source_target_pairs={{0,3},{1,2},{2,1},{3,0},{4,7},{5,6},{6,5},{7,4},{8,11},{9,10},{10,... | collective-permute-start | bytes 12296 | tf_op jit(solution)/shard_map/ppermute | solution.py:382
  21.6 2.4 %collective-permute-done.3 = f32[8,128]{1,0:T(8,128)S(1)} collective-permute-done((f32[8,128]{1,0:T(8,128)S(1)}, f32[8,128]{1,0:T(8,128)S(1)}, u32[]{:S(2)}, u32[]{:S(2)}) %collective-permute-start.3) | collective-permute-done | bytes 4128 | tf_op jit(solution)/shard_map/ppermute | solution.py:382
  24.0 1.0 %collective-permute-start.4 = (f32[8,128]{1,0:T(8,128)S(1)}, f32[8,128]{1,0:T(8,128)S(1)}, u32[]{:S(2)}, u32[]{:S(2)}) collective-permute-start(f32[8,128]{1,0:T(8,128)S(1)} %max.13), channel_id=1, source_target_pairs={{0,5},{1,4},{2,7},{3,6},{4,1},{5,0},{6,3},{7,2},{8,13},{9,12},{10,... | collective-permute-start | bytes 12296 | tf_op jit(solution)/shard_map/ppermute | solution.py:382
  25.0 2.0 %collective-permute-done.4 = f32[8,128]{1,0:T(8,128)S(1)} collective-permute-done((f32[8,128]{1,0:T(8,128)S(1)}, f32[8,128]{1,0:T(8,128)S(1)}, u32[]{:S(2)}, u32[]{:S(2)}) %collective-permute-start.4) | collective-permute-done | bytes 4128 | tf_op jit(solution)/shard_map/ppermute | solution.py:382
  27.0 1.8 %collective-permute-start.5 = (f32[8,128]{1,0:T(8,128)S(1)}, f32[8,128]{1,0:T(8,128)S(1)}, u32[]{:S(2)}, u32[]{:S(2)}) collective-permute-start(f32[8,128]{1,0:T(8,128)S(1)} %max.14), channel_id=1, source_target_pairs={{0,9},{1,8},{2,11},{3,10},{4,13},{5,12},{6,15},{7,14},{8,1},{9,0},... | collective-permute-start | bytes 12296 | tf_op jit(solution)/shard_map/ppermute | solution.py:382
  28.9 1.0 %finish.1 = (f32[3,16384]{1,0:T(4,128)}, f32[3,16384]{1,0:T(4,128)}) custom-call(s32[8,128]{1,0:T(8,128)S(1)} %get-tuple-element.13.plan_ref, f32[64,8,256]{2,1,0:T(8,128)S(1)} %get-tuple-element.19.moved_ref, f32[3,16384]{1,0:T(4,128)S(1)} %get-tuple-element.16.frac_ref), custom_call_target="tpu_custom_call" | custom-call | bytes 8000000 | tf_op jit(solution)/shard_map/finish/pallas_call | solution.py:442
  29.9 1.1 %collective-permute-done.5 = f32[8,128]{1,0:T(8,128)S(1)} collective-permute-done((f32[8,128]{1,0:T(8,128)S(1)}, f32[8,128]{1,0:T(8,128)S(1)}, u32[]{:S(2)}, u32[]{:S(2)}) %collective-permute-start.5) | collective-permute-done | bytes 4128 | tf_op jit(solution)/shard_map/ppermute | solution.py:382
  31.0 0.5 %slice.3 = f32[1,1]{1,0:T(1,128)} slice(f32[8,128]{1,0:T(8,128)S(1)} %add_divide_fusion), slice={[0:1], [0:1]} | slice | bytes 8 | tf_op jit(solution)/shard_map/slice | solution.py:455
  (4 shorter events, 0.0 us)
Async XLA Ops:
  5.9 7.7 %collective-permute-start.1 = (f32[8,32,128]{2,1,0:T(8,128)S(1)}, f32[8,32,128]{2,1,0:T(8,128)S(1)}, u32[]{:S(2)}, u32[]{:S(2)}) collective-permute-start(f32[8,32,128]{2,1,0:T(8,128)S(1)} %get-tuple-element.14.near_ref), channel_id=1, source_target_pairs={{0,1},{1,0},{2,3},{3,2},{4,5},{5,4},{6,7},{7,6},{8,9},{9,8},{10,11... | collective-permute-start | bytes 393224 | tf_op jit(solution)/shard_map/ppermute | solution.py:423
  6.5 9.2 %collective-permute-start = (f32[8,32,128]{2,1,0:T(8,128)S(1)}, f32[8,32,128]{2,1,0:T(8,128)S(1)}, u32[]{:S(2)}, u32[]{:S(2)}) collective-permute-start(f32[8,32,128]{2,1,0:T(8,128)S(1)} %get-tuple-element.15.far_ref), channel_id=1, source_target_pairs={{0,15},{1,2},{2,1},{3,4},{4,3},{5,6},{6,5},{7,8},{8,7},{9,10},{10,... | collective-permute-start | bytes 393224 | tf_op jit(solution)/shard_map/ppermute | solution.py:424
  19.7 1.2 %collective-permute-start.2 = (f32[8,128]{1,0:T(8,128)S(1)}, f32[8,128]{1,0:T(8,128)S(1)}, u32[]{:S(2)}, u32[]{:S(2)}) collective-permute-start(f32[8,128]{1,0:T(8,128)S(1)} %get-tuple-element.22), channel_id=1, source_target_pairs={{0,1},{1,0},{2,3},{3,2},{4,5},{5,4},{6,7},{7,6},{8,9},{9,8},{10,11... | collective-permute-start | bytes 12296 | tf_op jit(solution)/shard_map/ppermute | solution.py:382
  21.0 3.0 %collective-permute-start.3 = (f32[8,128]{1,0:T(8,128)S(1)}, f32[8,128]{1,0:T(8,128)S(1)}, u32[]{:S(2)}, u32[]{:S(2)}) collective-permute-start(f32[8,128]{1,0:T(8,128)S(1)} %max.12), channel_id=1, source_target_pairs={{0,3},{1,2},{2,1},{3,0},{4,7},{5,6},{6,5},{7,4},{8,11},{9,10},{10,... | collective-permute-start | bytes 12296 | tf_op jit(solution)/shard_map/ppermute | solution.py:382
  24.0 3.0 %collective-permute-start.4 = (f32[8,128]{1,0:T(8,128)S(1)}, f32[8,128]{1,0:T(8,128)S(1)}, u32[]{:S(2)}, u32[]{:S(2)}) collective-permute-start(f32[8,128]{1,0:T(8,128)S(1)} %max.13), channel_id=1, source_target_pairs={{0,5},{1,4},{2,7},{3,6},{4,1},{5,0},{6,3},{7,2},{8,13},{9,12},{10,... | collective-permute-start | bytes 12296 | tf_op jit(solution)/shard_map/ppermute | solution.py:382
  27.0 3.9 %collective-permute-start.5 = (f32[8,128]{1,0:T(8,128)S(1)}, f32[8,128]{1,0:T(8,128)S(1)}, u32[]{:S(2)}, u32[]{:S(2)}) collective-permute-start(f32[8,128]{1,0:T(8,128)S(1)} %max.14), channel_id=1, source_target_pairs={{0,9},{1,8},{2,11},{3,10},{4,13},{5,12},{6,15},{7,14},{8,1},{9,0},... | collective-permute-start | bytes 12296 | tf_op jit(solution)/shard_map/ppermute | solution.py:382

commit v2 on v1

--- a/solution.py
+++ b/solution.py
@@ -15,7 +15,7 @@
 LANES = 128
 UNROLL = 8
 GIVEN = 32
-TAKEN = 16
+TAKEN = 32
 SPREAD = 32
 TABLE = 16
 
@@ -163,9 +163,11 @@
             )
             found.append((listed_ref[1, v], both[:SPREAD] + both[SPREAD:]))
         for base, part in found:
-            for k, ahead in enumerate((0, 1, NY + 1, NY + 2)):
-                at = pl.ds(pl.multiple_of((base + ahead) * 8, 8), 8)
-                acc_ref[at, :] += part[8 * k : 8 * k + 8]
+            here = pl.ds(pl.multiple_of(base * 8, 8), 16)
+            above = pl.ds(pl.multiple_of(base * 8, 8) + (NY + 1) * 8, 16)
+            lower, upper = acc_ref[here, :], acc_ref[above, :]
+            acc_ref[here, :] = lower + part[:16]
+            acc_ref[above, :] = upper + part[16:]
         return carry
 
     lax.fori_loop(0, (total + GIVEN - 1) // GIVEN, visit, 0)

time: 31.9 us -> 31.5 us (0.987)
  waiting for transfers between devices: 8.66 us -> 7.88 us
    ppermute x1, starting transfers between devices: 6.56 us -> 5.06 us  [body(): far_new = lax.ppermute(far, 'gx', far_pairs)]
    ppermute x1, starting transfers between devices: 0.53 us -> 1.43 us  [body(): near_new = lax.ppermute(near, 'gx', near_pairs)]
    ppermute x4, starting transfers between devices: 3.55 us -> 4.4 us  [largest(): value = jnp.maximum(value, lax.ppermute(value, axis, pairs))]
    ppermute x4, waiting for transfers between devices: 6.67 us -> 5.89 us  [largest(): value = jnp.maximum(value, lax.ppermute(value, axis, pairs))]
where the time goes in v2:
time: 31.5 us; the launch traced here: 31 us
  starting transfers between devices  10.9 us (35%)
  Pallas kernels  9.77 us (31%)
  waiting for transfers between devices  7.88 us (25%)
  between operations  1.97 us (6%)
  local copies, waits for them, and re-layouts  0.52 us (2%)
    ppermute x4, waiting for transfers between devices, largest(): value = jnp.maximum(value, lax.ppermute(value, axis, pairs))  5.89 us
    ppermute x1, starting transfers between devices, body(): far_new = lax.ppermute(far, 'gx', far_pairs)  5.06 us
    pallas_call x1, Pallas kernels, body(): pl.pallas_call(spread_kernel, out_shape=(layer_pair, layer_pair, pltpu.VM...  4.64 us
    ppermute x4, starting transfers between devices, largest(): value = jnp.maximum(value, lax.ppermute(value, axis, pairs))  4.4 us
    pallas_call x1, Pallas kernels, body(): pl.pallas_call(collect_kernel, out_shape=(jax.ShapeDtypeStruct((blocks, 8...  4.13 us
    ppermute x1, waiting for transfers between devices, body(): far_new = lax.ppermute(far, 'gx', far_pairs)  1.99 us
    ppermute x1, starting transfers between devices, body(): near_new = lax.ppermute(near, 'gx', near_pairs)  1.43 us
    pallas_call x1, Pallas kernels, body(): pl.pallas_call(finish_kernel, out_shape=(jax.ShapeDtypeStruct(frac.shape,...  1 us
  transfers between devices with their start and end apart: 6, of which 5 were waited for; matrix products, arithmetic and copies ran while one was open for 0% of the time, Pallas kernels for 3%

profile of v2, /device:TPU:0, one launch (start us, length us, event | category | flops | bytes accessed | tf_op | source)
XLA Modules:
  0.0 31.0 jit_solution(15481793324064643471)
XLA Ops:
  1.3 4.6 %spread.1 = (f32[8,32,128]{2,1,0:T(8,128)S(1)}, f32[8,32,128]{2,1,0:T(8,128)S(1)}, s32[8,128]{1,0:T(8,128)S(1)}, f32[3,16384]{1,0:T(4,128)S(1)}, f32[3,16384]{1,0:T(4,128)S(1)}, /*index=5*/s32[128,128]{1,0:T(8,128)S(1)}) custom-call(s32[1]{0:T(128)S(6)} %copy.9.count_ref, f32[3,16384]{1,0:T(4,128)} %frac_hbm.1, f32[3,16384]{1,0:T(4,128)} %vel_hbm.1, ...), custom_call_target="tpu_custom_call" | custom-call | tf_op jit(solution)/shard_map/spread/pallas_call | solution.py:400
  5.9 1.4 %collective-permute-start.1 = (f32[8,32,128]{2,1,0:T(8,128)S(1)}, f32[8,32,128]{2,1,0:T(8,128)S(1)}, u32[]{:S(2)}, u32[]{:S(2)}) collective-permute-start(f32[8,32,128]{2,1,0:T(8,128)S(1)} %get-tuple-element.14.near_ref), channel_id=1, source_target_pairs={{0,1},{1,0},{2,3},{3,2},{4,5},{5,4},{6,7},{7,6},{8,9},{9,8},{10,11... | collective-permute-start | bytes 393224 | tf_op jit(solution)/shard_map/ppermute | solution.py:425
  7.4 5.1 %collective-permute-start = (f32[8,32,128]{2,1,0:T(8,128)S(1)}, f32[8,32,128]{2,1,0:T(8,128)S(1)}, u32[]{:S(2)}, u32[]{:S(2)}) collective-permute-start(f32[8,32,128]{2,1,0:T(8,128)S(1)} %get-tuple-element.15.far_ref), channel_id=1, source_target_pairs={{0,15},{1,2},{2,1},{3,4},{4,3},{5,6},{6,5},{7,8},{8,7},{9,10},{10,... | collective-permute-start | bytes 393224 | tf_op jit(solution)/shard_map/ppermute | solution.py:426
  13.1 0.0 collective-permute-done.1.near_new_ref
  13.1 2.0 %collective-permute-done.far_new_ref = f32[8,32,128]{2,1,0:T(8,128)S(1)} collective-permute-done((f32[8,32,128]{2,1,0:T(8,128)S(1)}, f32[8,32,128]{2,1,0:T(8,128)S(1)}, u32[]{:S(2)}, u32[]{:S(2)}) %collective-permute-start) | collective-permute-done | bytes 131104 | tf_op jit(solution)/shard_map/ppermute | solution.py:426
  15.1 4.1 %collect.1 = (f32[64,8,256]{2,1,0:T(8,128)S(1)}, f32[8,128]{1,0:T(8,128)S(1)}) custom-call(f32[1]{0:T(128)S(6)} %copy.10.step_ref, s32[8,128]{1,0:T(8,128)S(1)} %get-tuple-element.13.plan_ref, f32[8,32,128]{2,1,0:T(8,128)S(1)} %get-tuple-element.14.near_ref, f32[8,32,128]{2,1,0:T(8,128)S(1)} %get-tuple-element.15.far_ref, ...), custom_call_target="tpu_custom_call" | custom-call | tf_op jit(solution)/shard_map/collect/pallas_call | solution.py:427
  19.2 0.1 collective-permute-start.2
  19.3 1.2 %collective-permute-done.2 = f32[8,128]{1,0:T(8,128)S(1)} collective-permute-done((f32[8,128]{1,0:T(8,128)S(1)}, f32[8,128]{1,0:T(8,128)S(1)}, u32[]{:S(2)}, u32[]{:S(2)}) %collective-permute-start.2) | collective-permute-done | bytes 4128 | tf_op jit(solution)/shard_map/ppermute | solution.py:384
  20.4 0.0 collective-permute-start.3
  20.4 3.0 %collective-permute-done.3 = f32[8,128]{1,0:T(8,128)S(1)} collective-permute-done((f32[8,128]{1,0:T(8,128)S(1)}, f32[8,128]{1,0:T(8,128)S(1)}, u32[]{:S(2)}, u32[]{:S(2)}) %collective-permute-start.3) | collective-permute-done | bytes 4128 | tf_op jit(solution)/shard_map/ppermute | solution.py:384
  23.5 1.7 %collective-permute-start.4 = (f32[8,128]{1,0:T(8,128)S(1)}, f32[8,128]{1,0:T(8,128)S(1)}, u32[]{:S(2)}, u32[]{:S(2)}) collective-permute-start(f32[8,128]{1,0:T(8,128)S(1)} %max.13), channel_id=1, source_target_pairs={{0,5},{1,4},{2,7},{3,6},{4,1},{5,0},{6,3},{7,2},{8,13},{9,12},{10,... | collective-permute-start | bytes 12296 | tf_op jit(solution)/shard_map/ppermute | solution.py:384
  25.1 1.4 %collective-permute-done.4 = f32[8,128]{1,0:T(8,128)S(1)} collective-permute-done((f32[8,128]{1,0:T(8,128)S(1)}, f32[8,128]{1,0:T(8,128)S(1)}, u32[]{:S(2)}, u32[]{:S(2)}) %collective-permute-start.4) | collective-permute-done | bytes 4128 | tf_op jit(solution)/shard_map/ppermute | solution.py:384
  26.5 2.7 %collective-permute-start.5 = (f32[8,128]{1,0:T(8,128)S(1)}, f32[8,128]{1,0:T(8,128)S(1)}, u32[]{:S(2)}, u32[]{:S(2)}) collective-permute-start(f32[8,128]{1,0:T(8,128)S(1)} %max.14), channel_id=1, source_target_pairs={{0,9},{1,8},{2,11},{3,10},{4,13},{5,12},{6,15},{7,14},{8,1},{9,0},... | collective-permute-start | bytes 12296 | tf_op jit(solution)/shard_map/ppermute | solution.py:384
  29.2 1.0 %finish.1 = (f32[3,16384]{1,0:T(4,128)}, f32[3,16384]{1,0:T(4,128)}) custom-call(s32[8,128]{1,0:T(8,128)S(1)} %get-tuple-element.13.plan_ref, f32[64,8,256]{2,1,0:T(8,128)S(1)} %get-tuple-element.19.moved_ref, f32[3,16384]{1,0:T(4,128)S(1)} %get-tuple-element.16.frac_ref), custom_call_target="tpu_custom_call" | custom-call | bytes 8000000 | tf_op jit(solution)/shard_map/finish/pallas_call | solution.py:444
  30.2 0.3 %collective-permute-done.5 = f32[8,128]{1,0:T(8,128)S(1)} collective-permute-done((f32[8,128]{1,0:T(8,128)S(1)}, f32[8,128]{1,0:T(8,128)S(1)}, u32[]{:S(2)}, u32[]{:S(2)}) %collective-permute-start.5) | collective-permute-done | bytes 4128 | tf_op jit(solution)/shard_map/ppermute | solution.py:384
  30.5 0.5 %slice.3 = f32[1,1]{1,0:T(1,128)} slice(f32[8,128]{1,0:T(8,128)S(1)} %add_divide_fusion), slice={[0:1], [0:1]} | slice | bytes 8 | tf_op jit(solution)/shard_map/slice | solution.py:457
  (4 shorter events, 0.0 us)
Async XLA Ops:
  5.9 7.1 %collective-permute-start.1 = (f32[8,32,128]{2,1,0:T(8,128)S(1)}, f32[8,32,128]{2,1,0:T(8,128)S(1)}, u32[]{:S(2)}, u32[]{:S(2)}) collective-permute-start(f32[8,32,128]{2,1,0:T(8,128)S(1)} %get-tuple-element.14.near_ref), channel_id=1, source_target_pairs={{0,1},{1,0},{2,3},{3,2},{4,5},{5,4},{6,7},{7,6},{8,9},{9,8},{10,11... | collective-permute-start | bytes 393224 | tf_op jit(solution)/shard_map/ppermute | solution.py:425
  7.4 7.7 %collective-permute-start = (f32[8,32,128]{2,1,0:T(8,128)S(1)}, f32[8,32,128]{2,1,0:T(8,128)S(1)}, u32[]{:S(2)}, u32[]{:S(2)}) collective-permute-start(f32[8,32,128]{2,1,0:T(8,128)S(1)} %get-tuple-element.15.far_ref), channel_id=1, source_target_pairs={{0,15},{1,2},{2,1},{3,4},{4,3},{5,6},{6,5},{7,8},{8,7},{9,10},{10,... | collective-permute-start | bytes 393224 | tf_op jit(solution)/shard_map/ppermute | solution.py:426
  19.2 1.2 %collective-permute-start.2 = (f32[8,128]{1,0:T(8,128)S(1)}, f32[8,128]{1,0:T(8,128)S(1)}, u32[]{:S(2)}, u32[]{:S(2)}) collective-permute-start(f32[8,128]{1,0:T(8,128)S(1)} %get-tuple-element.22), channel_id=1, source_target_pairs={{0,1},{1,0},{2,3},{3,2},{4,5},{5,4},{6,7},{7,6},{8,9},{9,8},{10,11... | collective-permute-start | bytes 12296 | tf_op jit(solution)/shard_map/ppermute | solution.py:384
  20.4 3.0 %collective-permute-start.3 = (f32[8,128]{1,0:T(8,128)S(1)}, f32[8,128]{1,0:T(8,128)S(1)}, u32[]{:S(2)}, u32[]{:S(2)}) collective-permute-start(f32[8,128]{1,0:T(8,128)S(1)} %max.12), channel_id=1, source_target_pairs={{0,3},{1,2},{2,1},{3,0},{4,7},{5,6},{6,5},{7,4},{8,11},{9,10},{10,... | collective-permute-start | bytes 12296 | tf_op jit(solution)/shard_map/ppermute | solution.py:384
  23.5 3.0 %collective-permute-start.4 = (f32[8,128]{1,0:T(8,128)S(1)}, f32[8,128]{1,0:T(8,128)S(1)}, u32[]{:S(2)}, u32[]{:S(2)}) collective-permute-start(f32[8,128]{1,0:T(8,128)S(1)} %max.13), channel_id=1, source_target_pairs={{0,5},{1,4},{2,7},{3,6},{4,1},{5,0},{6,3},{7,2},{8,13},{9,12},{10,... | collective-permute-start | bytes 12296 | tf_op jit(solution)/shard_map/ppermute | solution.py:384
  26.5 4.0 %collective-permute-start.5 = (f32[8,128]{1,0:T(8,128)S(1)}, f32[8,128]{1,0:T(8,128)S(1)}, u32[]{:S(2)}, u32[]{:S(2)}) collective-permute-start(f32[8,128]{1,0:T(8,128)S(1)} %max.14), channel_id=1, source_target_pairs={{0,9},{1,8},{2,11},{3,10},{4,13},{5,12},{6,15},{7,14},{8,1},{9,0},... | collective-permute-start | bytes 12296 | tf_op jit(solution)/shard_map/ppermute | solution.py:384

commit v3 on v2

--- a/solution.py
+++ b/solution.py
@@ -45,15 +45,15 @@
 def one_hot(cells_ref, block, offset):
     rel = cells_ref[pl.ds(block * 2, 2), :] - offset
     tall = (16, LANES)
-    nodes = lax.broadcasted_iota(jnp.int32, tall, 0).astype(jnp.int16)
+    nodes = lax.broadcasted_iota(jnp.int32, tall, 0).astype(f32)
     one, zero = jnp.ones(tall, bf16), jnp.zeros(tall, bf16)
     halves = []
     for h in range(2):
-        line = jnp.broadcast_to(rel[h : h + 1, :], tall).astype(jnp.int16)
+        line = jnp.broadcast_to(rel[h : h + 1, :].astype(f32), tall).astype(bf16)
         halves.append(
             jnp.concatenate(
                 [
-                    jnp.where(line == nodes + jnp.int16(z), one, zero)
+                    jnp.where(line == (nodes + z).astype(bf16), one, zero)
                     for z in range(0, NZ, 16)
                 ],
                 axis=0,

time: 31.5 us -> 31.7 us (level)
  waiting for transfers between devices: 7.88 us -> 10.3 us
  starting transfers between devices: 10.9 us -> 9 us
    ppermute x4, starting transfers between devices: 4.4 us -> 1.93 us  [largest(): value = jnp.maximum(value, lax.ppermute(value, axis, pairs))]
    ppermute x4, waiting for transfers between devices: 5.89 us -> 8.29 us  [largest(): value = jnp.maximum(value, lax.ppermute(value, axis, pairs))]
    ppermute x1, starting transfers between devices: 5.06 us -> 6.55 us  [body(): far_new = lax.ppermute(far, 'gx', far_pairs)]
    ppermute x1, starting transfers between devices: 1.43 us -> 0.52 us  [body(): near_new = lax.ppermute(near, 'gx', near_pairs)]
where the time goes in v3:
time: 31.7 us; the launch traced here: 31.5 us
  waiting for transfers between devices  10.3 us (32%)
  Pallas kernels  9.73 us (31%)
  starting transfers between devices  9 us (28%)
  between operations  1.97 us (6%)
  local copies, waits for them, and re-layouts  0.52 us (2%)
    ppermute x4, waiting for transfers between devices, largest(): value = jnp.maximum(value, lax.ppermute(value, axis, pairs))  8.29 us
    ppermute x1, starting transfers between devices, body(): far_new = lax.ppermute(far, 'gx', far_pairs)  6.55 us
    pallas_call x1, Pallas kernels, body(): pl.pallas_call(spread_kernel, out_shape=(layer_pair, layer_pair, pltpu.VM...  4.61 us
    pallas_call x1, Pallas kernels, body(): pl.pallas_call(collect_kernel, out_shape=(jax.ShapeDtypeStruct((blocks, 8...  4.12 us
    ppermute x1, waiting for transfers between devices, body(): far_new = lax.ppermute(far, 'gx', far_pairs)  1.99 us
    ppermute x4, starting transfers between devices, largest(): value = jnp.maximum(value, lax.ppermute(value, axis, pairs))  1.93 us
    pallas_call x1, Pallas kernels, body(): pl.pallas_call(finish_kernel, out_shape=(jax.ShapeDtypeStruct(frac.shape,...  1 us
  transfers between devices with their start and end apart: 6, of which 5 were waited for; matrix products, arithmetic and copies ran while one was open for 0% of the time, Pallas kernels for 3%

profile of v3, /device:TPU:0, one launch (start us, length us, event | category | flops | bytes accessed | tf_op | source)
XLA Modules:
  0.0 31.5 jit_solution(5477355044107017551)
XLA Ops:
  1.3 4.6 %spread.1 = (f32[8,32,128]{2,1,0:T(8,128)S(1)}, f32[8,32,128]{2,1,0:T(8,128)S(1)}, s32[8,128]{1,0:T(8,128)S(1)}, f32[3,16384]{1,0:T(4,128)S(1)}, f32[3,16384]{1,0:T(4,128)S(1)}, /*index=5*/s32[128,128]{1,0:T(8,128)S(1)}) custom-call(s32[1]{0:T(128)S(6)} %copy.9.count_ref, f32[3,16384]{1,0:T(4,128)} %frac_hbm.1, f32[3,16384]{1,0:T(4,128)} %vel_hbm.1, ...), custom_call_target="tpu_custom_call" | custom-call | tf_op jit(solution)/shard_map/spread/pallas_call | solution.py:400
  5.9 0.5 %collective-permute-start.1 = (f32[8,32,128]{2,1,0:T(8,128)S(1)}, f32[8,32,128]{2,1,0:T(8,128)S(1)}, u32[]{:S(2)}, u32[]{:S(2)}) collective-permute-start(f32[8,32,128]{2,1,0:T(8,128)S(1)} %get-tuple-element.14.near_ref), channel_id=1, source_target_pairs={{0,1},{1,0},{2,3},{3,2},{4,5},{5,4},{6,7},{7,6},{8,9},{9,8},{10,11... | collective-permute-start | bytes 393224 | tf_op jit(solution)/shard_map/ppermute | solution.py:425
  6.4 6.5 %collective-permute-start = (f32[8,32,128]{2,1,0:T(8,128)S(1)}, f32[8,32,128]{2,1,0:T(8,128)S(1)}, u32[]{:S(2)}, u32[]{:S(2)}) collective-permute-start(f32[8,32,128]{2,1,0:T(8,128)S(1)} %get-tuple-element.15.far_ref), channel_id=1, source_target_pairs={{0,15},{1,2},{2,1},{3,4},{4,3},{5,6},{6,5},{7,8},{8,7},{9,10},{10,... | collective-permute-start | bytes 393224 | tf_op jit(solution)/shard_map/ppermute | solution.py:426
  13.6 0.0 collective-permute-done.1.near_new_ref
  13.6 2.0 %collective-permute-done.far_new_ref = f32[8,32,128]{2,1,0:T(8,128)S(1)} collective-permute-done((f32[8,32,128]{2,1,0:T(8,128)S(1)}, f32[8,32,128]{2,1,0:T(8,128)S(1)}, u32[]{:S(2)}, u32[]{:S(2)}) %collective-permute-start) | collective-permute-done | bytes 131104 | tf_op jit(solution)/shard_map/ppermute | solution.py:426
  15.6 4.1 %collect.1 = (f32[64,8,256]{2,1,0:T(8,128)S(1)}, f32[8,128]{1,0:T(8,128)S(1)}) custom-call(f32[1]{0:T(128)S(6)} %copy.10.step_ref, s32[8,128]{1,0:T(8,128)S(1)} %get-tuple-element.13.plan_ref, f32[8,32,128]{2,1,0:T(8,128)S(1)} %get-tuple-element.14.near_ref, f32[8,32,128]{2,1,0:T(8,128)S(1)} %get-tuple-element.15.far_ref, ...), custom_call_target="tpu_custom_call" | custom-call | tf_op jit(solution)/shard_map/collect/pallas_call | solution.py:427
  19.7 0.1 collective-permute-start.2
  19.8 1.2 %collective-permute-done.2 = f32[8,128]{1,0:T(8,128)S(1)} collective-permute-done((f32[8,128]{1,0:T(8,128)S(1)}, f32[8,128]{1,0:T(8,128)S(1)}, u32[]{:S(2)}, u32[]{:S(2)}) %collective-permute-start.2) | collective-permute-done | bytes 4128 | tf_op jit(solution)/shard_map/ppermute | solution.py:384
  21.0 0.0 collective-permute-start.3
  21.0 3.0 %collective-permute-done.3 = f32[8,128]{1,0:T(8,128)S(1)} collective-permute-done((f32[8,128]{1,0:T(8,128)S(1)}, f32[8,128]{1,0:T(8,128)S(1)}, u32[]{:S(2)}, u32[]{:S(2)}) %collective-permute-start.3) | collective-permute-done | bytes 4128 | tf_op jit(solution)/shard_map/ppermute | solution.py:384
  24.0 0.0 collective-permute-start.4
  24.0 3.0 %collective-permute-done.4 = f32[8,128]{1,0:T(8,128)S(1)} collective-permute-done((f32[8,128]{1,0:T(8,128)S(1)}, f32[8,128]{1,0:T(8,128)S(1)}, u32[]{:S(2)}, u32[]{:S(2)}) %collective-permute-start.4) | collective-permute-done | bytes 4128 | tf_op jit(solution)/shard_map/ppermute | solution.py:384
  27.1 1.9 %collective-permute-start.5 = (f32[8,128]{1,0:T(8,128)S(1)}, f32[8,128]{1,0:T(8,128)S(1)}, u32[]{:S(2)}, u32[]{:S(2)}) collective-permute-start(f32[8,128]{1,0:T(8,128)S(1)} %max.14), channel_id=1, source_target_pairs={{0,9},{1,8},{2,11},{3,10},{4,13},{5,12},{6,15},{7,14},{8,1},{9,0},... | collective-permute-start | bytes 12296 | tf_op jit(solution)/shard_map/ppermute | solution.py:384
  28.9 1.0 %finish.1 = (f32[3,16384]{1,0:T(4,128)}, f32[3,16384]{1,0:T(4,128)}) custom-call(s32[8,128]{1,0:T(8,128)S(1)} %get-tuple-element.13.plan_ref, f32[64,8,256]{2,1,0:T(8,128)S(1)} %get-tuple-element.19.moved_ref, f32[3,16384]{1,0:T(4,128)S(1)} %get-tuple-element.16.frac_ref), custom_call_target="tpu_custom_call" | custom-call | bytes 8000000 | tf_op jit(solution)/shard_map/finish/pallas_call | solution.py:444
  29.9 1.1 %collective-permute-done.5 = f32[8,128]{1,0:T(8,128)S(1)} collective-permute-done((f32[8,128]{1,0:T(8,128)S(1)}, f32[8,128]{1,0:T(8,128)S(1)}, u32[]{:S(2)}, u32[]{:S(2)}) %collective-permute-start.5) | collective-permute-done | bytes 4128 | tf_op jit(solution)/shard_map/ppermute | solution.py:384
  31.0 0.5 %slice.3 = f32[1,1]{1,0:T(1,128)} slice(f32[8,128]{1,0:T(8,128)S(1)} %add_divide_fusion), slice={[0:1], [0:1]} | slice | bytes 8 | tf_op jit(solution)/shard_map/slice | solution.py:457
  (4 shorter events, 0.0 us)
Async XLA Ops:
  5.9 7.7 %collective-permute-start.1 = (f32[8,32,128]{2,1,0:T(8,128)S(1)}, f32[8,32,128]{2,1,0:T(8,128)S(1)}, u32[]{:S(2)}, u32[]{:S(2)}) collective-permute-start(f32[8,32,128]{2,1,0:T(8,128)S(1)} %get-tuple-element.14.near_ref), channel_id=1, source_target_pairs={{0,1},{1,0},{2,3},{3,2},{4,5},{5,4},{6,7},{7,6},{8,9},{9,8},{10,11... | collective-permute-start | bytes 393224 | tf_op jit(solution)/shard_map/ppermute | solution.py:425
  6.4 9.2 %collective-permute-start = (f32[8,32,128]{2,1,0:T(8,128)S(1)}, f32[8,32,128]{2,1,0:T(8,128)S(1)}, u32[]{:S(2)}, u32[]{:S(2)}) collective-permute-start(f32[8,32,128]{2,1,0:T(8,128)S(1)} %get-tuple-element.15.far_ref), channel_id=1, source_target_pairs={{0,15},{1,2},{2,1},{3,4},{4,3},{5,6},{6,5},{7,8},{8,7},{9,10},{10,... | collective-permute-start | bytes 393224 | tf_op jit(solution)/shard_map/ppermute | solution.py:426
  19.7 1.2 %collective-permute-start.2 = (f32[8,128]{1,0:T(8,128)S(1)}, f32[8,128]{1,0:T(8,128)S(1)}, u32[]{:S(2)}, u32[]{:S(2)}) collective-permute-start(f32[8,128]{1,0:T(8,128)S(1)} %get-tuple-element.22), channel_id=1, source_target_pairs={{0,1},{1,0},{2,3},{3,2},{4,5},{5,4},{6,7},{7,6},{8,9},{9,8},{10,11... | collective-permute-start | bytes 12296 | tf_op jit(solution)/shard_map/ppermute | solution.py:384
  21.0 3.0 %collective-permute-start.3 = (f32[8,128]{1,0:T(8,128)S(1)}, f32[8,128]{1,0:T(8,128)S(1)}, u32[]{:S(2)}, u32[]{:S(2)}) collective-permute-start(f32[8,128]{1,0:T(8,128)S(1)} %max.12), channel_id=1, source_target_pairs={{0,3},{1,2},{2,1},{3,0},{4,7},{5,6},{6,5},{7,4},{8,11},{9,10},{10,... | collective-permute-start | bytes 12296 | tf_op jit(solution)/shard_map/ppermute | solution.py:384
  24.0 3.0 %collective-permute-start.4 = (f32[8,128]{1,0:T(8,128)S(1)}, f32[8,128]{1,0:T(8,128)S(1)}, u32[]{:S(2)}, u32[]{:S(2)}) collective-permute-start(f32[8,128]{1,0:T(8,128)S(1)} %max.13), channel_id=1, source_target_pairs={{0,5},{1,4},{2,7},{3,6},{4,1},{5,0},{6,3},{7,2},{8,13},{9,12},{10,... | collective-permute-start | bytes 12296 | tf_op jit(solution)/shard_map/ppermute | solution.py:384
  27.1 3.9 %collective-permute-start.5 = (f32[8,128]{1,0:T(8,128)S(1)}, f32[8,128]{1,0:T(8,128)S(1)}, u32[]{:S(2)}, u32[]{:S(2)}) collective-permute-start(f32[8,128]{1,0:T(8,128)S(1)} %max.14), channel_id=1, source_target_pairs={{0,9},{1,8},{2,11},{3,10},{4,13},{5,12},{6,15},{7,14},{8,1},{9,0},... | collective-permute-start | bytes 12296 | tf_op jit(solution)/shard_map/ppermute | solution.py:384

commit v4 on v3

--- a/solution.py
+++ b/solution.py
@@ -93,8 +93,8 @@
 
 def spread_kernel(
     count_ref, frac_hbm, vel_hbm, mass_hbm, cells_hbm,
-    far_ref, near_ref, plan_ref, frac_ref, vel_ref, cells_ref,
-    listed_ref, mass_ref, q_ref, acc_ref, sems,
+    far_ref, near_ref, layers_ref, plan_ref, frac_ref, vel_ref, hot_ref,
+    cells_ref, listed_ref, mass_ref, q_ref, acc_ref, sems,
 ):
     slots = frac_ref.shape[1]
     sources = (cells_hbm, frac_hbm, vel_hbm, mass_hbm)
@@ -154,6 +154,7 @@
             v = group * GIVEN + u
             block = listed_ref[0, v]
             hot = one_hot(cells_ref, block, listed_ref[2, v])
+            hot_ref[pl.ds(v, 1)] = hot[None]
             both = q_ref[pl.ds(block * 2, 2)]
             both = lax.dot_general(
                 jnp.concatenate([both[0], both[1]], axis=1),
@@ -172,6 +173,7 @@
 
     lax.fori_loop(0, (total + GIVEN - 1) // GIVEN, visit, 0)
 
+    odd = lax.axis_index("gx") % 2 == 1
     layers = []
     for l in range(CX + 1):
         first = l * (NY + 1) * 8
@@ -180,12 +182,10 @@
             lower = acc_ref[pl.ds(first + f, NY, stride=8), :]
             upper = acc_ref[pl.ds(first + 4 + f, NY, stride=8), :]
             layers.append(lower + pltpu.roll(upper, 1, 1))
-    odd = lax.axis_index("gx") % 2 == 1
-    for l in range(CX):
-        for f in range(4):
-            low, high = layers[l * 4 + f], layers[(l + 1) * 4 + f]
-            near_ref[f * CX + l] = jnp.where(odd, low, high)
-            far_ref[f * CX + l] = jnp.where(odd, high, low)
+            layers_ref[l * 4 + f] = layers[-1]
+    for k in range(CX * 4):
+        far_ref[k] = jnp.where(odd, layers[k + 4], layers[k])
+        near_ref[k] = jnp.where(odd, layers[k], layers[k + 4])
 
 
 def pair_up(field, axis):
@@ -252,7 +252,7 @@
 
 
 def collect_kernel(
-    step_ref, plan_ref, near_ref, far_ref, far_new_ref, near_new_ref, frac_ref, vel_ref, cells_ref,
+    step_ref, plan_ref, layers_ref, far_new_ref, near_new_ref, frac_ref, vel_ref, hot_ref,
     out_ref, top_ref, listed_ref, tab_ref, pair_ref, sem,
 ):
     blocks = frac_ref.shape[1] // BLOCK
@@ -264,14 +264,14 @@
     def pick(if_odd, if_even):
         return [jnp.where(odd, if_odd[k], if_even[k]) for k in range(4 * CX)]
 
-    low, high = pick(near_ref, far_ref), pick(far_ref, near_ref)
+    own = [layers_ref[k] for k in range(4 * (CX + 1))]
     left, right = pick(near_new_ref, far_new_ref), pick(far_new_ref, near_new_ref)
     nodes = [
-        [left[f * 2] for f in range(4)],
-        [low[f * 2] + left[f * 2 + 1] for f in range(4)],
-        [low[f * 2 + 1] for f in range(4)],
-        [high[f * 2 + 1] + right[f * 2] for f in range(4)],
-        [right[f * 2 + 1] for f in range(4)],
+        left[:4],
+        [own[f] + left[4 + f] for f in range(4)],
+        own[4:8],
+        [own[8 + f] + right[f] for f in range(4)],
+        right[4:],
     ]
     height = lax.broadcasted_iota(jnp.int32, (NY, NZ), 1)
     keep = height < NZ - 1
@@ -318,7 +318,7 @@
             v = group * TAKEN + u
             block = listed_ref[0, v]
             base = listed_ref[1, v]
-            hot = one_hot(cells_ref, block, listed_ref[2, v])
+            hot = hot_ref[pl.ds(v, 1)][0]
             rows = [pair_ref[base + ahead] for ahead in (0, 1, NY + 1, NY + 2)]
             value = jnp.dot(
                 jnp.concatenate(rows, axis=0),
@@ -396,20 +396,21 @@
     blocks = slots // BLOCK
     rows = slots // LANES
     inputs = (frac, velocity, mass.reshape(rows, LANES), particle_cell.reshape(rows, LANES))
-    layer_pair = pltpu.VMEM((4 * CX, NY, NZ), f32)
-    far, near, plan, frac_here, vel_here, cells_here = pl.pallas_call(
+    far, near, layers, plan, frac_here, vel_here, hots = pl.pallas_call(
         spread_kernel,
         out_shape=(
-            layer_pair,
-            layer_pair,
+            pltpu.VMEM((4 * CX, NY, NZ), f32),
+            pltpu.VMEM((4 * CX, NY, NZ), f32),
+            pltpu.VMEM((4 * (CX + 1), NY, NZ), f32),
             pltpu.VMEM((8, LANES), jnp.int32),
             pltpu.VMEM(frac.shape, f32),
             pltpu.VMEM(velocity.shape, f32),
-            pltpu.VMEM((rows, LANES), jnp.int32),
+            pltpu.VMEM((blocks + ROWS, NZ, BLOCK), bf16),
         ),
         in_specs=[smem] + [hbm] * 4,
-        out_specs=(vmem,) * 6,
+        out_specs=(vmem,) * 7,
         scratch_shapes=[
+            pltpu.VMEM((rows, LANES), jnp.int32),
             pltpu.SMEM((8, LANES), jnp.int32),
             pltpu.VMEM((rows, LANES), f32),
             pltpu.VMEM((rows, 2 * SPREAD, LANES), bf16),
@@ -422,15 +423,15 @@
     devices = lax.axis_size("gx")
     far_pairs = [(i, (i + (1 if i % 2 else -1)) % devices) for i in range(devices)]
     near_pairs = [(i, i ^ 1) for i in range(devices)]
+    far_new = lax.ppermute(far, "gx", far_pairs)
     near_new = lax.ppermute(near, "gx", near_pairs)
-    far_new = lax.ppermute(far, "gx", far_pairs)
     moved, top = pl.pallas_call(
         collect_kernel,
         out_shape=(
             jax.ShapeDtypeStruct((blocks, 8, BLOCK), f32),
             jax.ShapeDtypeStruct((8, LANES), f32),
         ),
-        in_specs=[smem] + [vmem] * 8,
+        in_specs=[smem] + [vmem] * 7,
         out_specs=(vmem, vmem),
         scratch_shapes=[
             pltpu.SMEM((8, LANES), jnp.int32),
@@ -440,7 +441,7 @@
         ],
         compiler_params=pltpu.CompilerParams(vmem_limit_bytes=32 * 1024 * 1024),
         name="collect",
-    )(time_step, plan, near, far, far_new, near_new, frac_here, vel_here, cells_here)
+    )(time_step, plan, layers, far_new, near_new, frac_here, vel_here, hots)
     new_frac, new_velocity = pl.pallas_call(
         finish_kernel,
         out_shape=(

time: 31.7 us -> 31.1 us (0.981)
  waiting for transfers between devices: 10.3 us -> 8.02 us
  Pallas kernels: 9.73 us -> 11.5 us
    ppermute x4, starting transfers between devices: 1.93 us -> 4.31 us  [largest(): value = jnp.maximum(value, lax.ppermute(value, axis, pairs))]
    ppermute x4, waiting for transfers between devices: 8.29 us -> 5.91 us  [largest(): value = jnp.maximum(value, lax.ppermute(value, axis, pairs))]
    ppermute x1, starting transfers between devices: 6.55 us -> 4.61 us  [body(): far_new = lax.ppermute(far, 'gx', far_pairs)]
    pallas_call x1, Pallas kernels: 4.61 us -> 5.52 us  [body(): pl.pallas_call(spread_kernel, out_shape=(pltpu.VMEM((4 * CX, NY, NZ), f32...]
    pallas_call x1, Pallas kernels: 4.12 us -> 5.01 us  [body(): pl.pallas_call(collect_kernel, out_shape=(jax.ShapeDtypeStruct((blocks, 8...]
    ppermute x1, starting transfers between devices: 0.52 us -> 0.01 us  [body(): near_new = lax.ppermute(near, 'gx', near_pairs)]
where the time goes in v4:
time: 31.1 us; the launch traced here: 31 us
  Pallas kernels  11.5 us (37%)
  starting transfers between devices  8.92 us (29%)
  waiting for transfers between devices  8.02 us (26%)
  between operations  1.96 us (6%)
  local copies, waits for them, and re-layouts  0.52 us (2%)
    ppermute x4, waiting for transfers between devices, largest(): value = jnp.maximum(value, lax.ppermute(value, axis, pairs))  5.91 us
    pallas_call x1, Pallas kernels, body(): pl.pallas_call(spread_kernel, out_shape=(pltpu.VMEM((4 * CX, NY, NZ), f32...  5.52 us
    pallas_call x1, Pallas kernels, body(): pl.pallas_call(collect_kernel, out_shape=(jax.ShapeDtypeStruct((blocks, 8...  5.01 us
    ppermute x1, starting transfers between devices, body(): far_new = lax.ppermute(far, 'gx', far_pairs)  4.61 us
    ppermute x4, starting transfers between devices, largest(): value = jnp.maximum(value, lax.ppermute(value, axis, pairs))  4.31 us
    ppermute x1, waiting for transfers between devices, body(): far_new = lax.ppermute(far, 'gx', far_pairs)  2.11 us
    pallas_call x1, Pallas kernels, body(): pl.pallas_call(finish_kernel, out_shape=(jax.ShapeDtypeStruct(frac.shape,...  1 us
  transfers between devices with their start and end apart: 6, of which 5 were waited for; matrix products, arithmetic and copies ran while one was open for 0% of the time, Pallas kernels for 3%

profile of v4, /device:TPU:0, one launch (start us, length us, event | category | flops | bytes accessed | tf_op | source)
XLA Modules:
  0.0 31.0 jit_solution(16552778866629679326)
XLA Ops:
  1.3 5.5 %spread.1 = (f32[8,32,128]{2,1,0:T(8,128)S(1)}, f32[8,32,128]{2,1,0:T(8,128)S(1)}, f32[12,32,128]{2,1,0:T(8,128)S(1)}, s32[8,128]{1,0:T(8,128)S(1)}, f32[3,16384...) custom-call(s32[1]{0:T(128)S(6)} %copy.9.count_ref, f32[3,16384]{1,0:T(4,128)} %frac_hbm.1, ...), custom_call_target="tpu_custom_call" | custom-call | tf_op jit(solution)/shard_map/spread/pallas_call | solution.py:399
  6.8 4.6 %collective-permute-start = (f32[8,32,128]{2,1,0:T(8,128)S(1)}, f32[8,32,128]{2,1,0:T(8,128)S(1)}, u32[]{:S(2)}, u32[]{:S(2)}) collective-permute-start(f32[8,32,128]{2,1,0:T(8,128)S(1)} %get-tuple-element.16), channel_id=1, source_target_pairs={{0,15},{1,2},{2,1},{3,4},{4,3},{5,6},{6,5},{7,8},{8,7},{9,10},{10,... | collective-permute-start | bytes 393224 | tf_op jit(solution)/shard_map/ppermute | solution.py:426
  11.4 0.0 collective-permute-start.1
  12.1 2.1 %collective-permute-done.far_new_ref = f32[8,32,128]{2,1,0:T(8,128)S(1)} collective-permute-done((f32[8,32,128]{2,1,0:T(8,128)S(1)}, f32[8,32,128]{2,1,0:T(8,128)S(1)}, u32[]{:S(2)}, u32[]{:S(2)}) %collective-permute-start) | collective-permute-done | bytes 131104 | tf_op jit(solution)/shard_map/ppermute | solution.py:426
  14.2 0.0 collective-permute-done.1.near_new_ref
  14.2 5.0 %collect.1 = (f32[64,8,256]{2,1,0:T(8,128)S(1)}, f32[8,128]{1,0:T(8,128)S(1)}) custom-call(f32[1]{0:T(128)S(6)} %copy.10.step_ref, s32[8,128]{1,0:T(8,128)S(1)} %get-tuple-element.14.plan_ref, f32[12,32,128]{2,1,0:T(8,128)S(1)} %get-tuple-element.15.layers_ref, f32[8,32,128]{2,1,0:T(8,128)S(1)} %collective-permute-done.far_new_ref, ...), custom_call_target="tpu_custom_call" | custom-call | tf_op jit(solution)/shard_map/collect/pallas_call | solution.py:428
  19.2 0.1 collective-permute-start.2
  19.3 1.2 %collective-permute-done.2 = f32[8,128]{1,0:T(8,128)S(1)} collective-permute-done((f32[8,128]{1,0:T(8,128)S(1)}, f32[8,128]{1,0:T(8,128)S(1)}, u32[]{:S(2)}, u32[]{:S(2)}) %collective-permute-start.2) | collective-permute-done | bytes 4128 | tf_op jit(solution)/shard_map/ppermute | solution.py:384
  20.4 1.2 %collective-permute-start.3 = (f32[8,128]{1,0:T(8,128)S(1)}, f32[8,128]{1,0:T(8,128)S(1)}, u32[]{:S(2)}, u32[]{:S(2)}) collective-permute-start(f32[8,128]{1,0:T(8,128)S(1)} %max.12), channel_id=1, source_target_pairs={{0,3},{1,2},{2,1},{3,0},{4,7},{5,6},{6,5},{7,4},{8,11},{9,10},{10,... | collective-permute-start | bytes 12296 | tf_op jit(solution)/shard_map/ppermute | solution.py:384
  21.7 1.8 %collective-permute-done.3 = f32[8,128]{1,0:T(8,128)S(1)} collective-permute-done((f32[8,128]{1,0:T(8,128)S(1)}, f32[8,128]{1,0:T(8,128)S(1)}, u32[]{:S(2)}, u32[]{:S(2)}) %collective-permute-start.3) | collective-permute-done | bytes 4128 | tf_op jit(solution)/shard_map/ppermute | solution.py:384
  23.5 1.0 %collective-permute-start.4 = (f32[8,128]{1,0:T(8,128)S(1)}, f32[8,128]{1,0:T(8,128)S(1)}, u32[]{:S(2)}, u32[]{:S(2)}) collective-permute-start(f32[8,128]{1,0:T(8,128)S(1)} %max.13), channel_id=1, source_target_pairs={{0,5},{1,4},{2,7},{3,6},{4,1},{5,0},{6,3},{7,2},{8,13},{9,12},{10,... | collective-permute-start | bytes 12296 | tf_op jit(solution)/shard_map/ppermute | solution.py:384
  24.5 2.0 %collective-permute-done.4 = f32[8,128]{1,0:T(8,128)S(1)} collective-permute-done((f32[8,128]{1,0:T(8,128)S(1)}, f32[8,128]{1,0:T(8,128)S(1)}, u32[]{:S(2)}, u32[]{:S(2)}) %collective-permute-start.4) | collective-permute-done | bytes 4128 | tf_op jit(solution)/shard_map/ppermute | solution.py:384
  26.5 2.0 %collective-permute-start.5 = (f32[8,128]{1,0:T(8,128)S(1)}, f32[8,128]{1,0:T(8,128)S(1)}, u32[]{:S(2)}, u32[]{:S(2)}) collective-permute-start(f32[8,128]{1,0:T(8,128)S(1)} %max.14), channel_id=1, source_target_pairs={{0,9},{1,8},{2,11},{3,10},{4,13},{5,12},{6,15},{7,14},{8,1},{9,0},... | collective-permute-start | bytes 12296 | tf_op jit(solution)/shard_map/ppermute | solution.py:384
  28.5 1.0 %finish.1 = (f32[3,16384]{1,0:T(4,128)}, f32[3,16384]{1,0:T(4,128)}) custom-call(s32[8,128]{1,0:T(8,128)S(1)} %get-tuple-element.14.plan_ref, f32[64,8,256]{2,1,0:T(8,128)S(1)} %get-tuple-element.21.moved_ref, f32[3,16384]{1,0:T(4,128)S(1)} %get-tuple-element.18.frac_ref), custom_call_target="tpu_custom_call" | custom-call | bytes 8000000 | tf_op jit(solution)/shard_map/finish/pallas_call | solution.py:445
  29.5 0.9 %collective-permute-done.5 = f32[8,128]{1,0:T(8,128)S(1)} collective-permute-done((f32[8,128]{1,0:T(8,128)S(1)}, f32[8,128]{1,0:T(8,128)S(1)}, u32[]{:S(2)}, u32[]{:S(2)}) %collective-permute-start.5) | collective-permute-done | bytes 4128 | tf_op jit(solution)/shard_map/ppermute | solution.py:384
  30.4 0.5 %slice.3 = f32[1,1]{1,0:T(1,128)} slice(f32[8,128]{1,0:T(8,128)S(1)} %add_divide_fusion), slice={[0:1], [0:1]} | slice | bytes 8 | tf_op jit(solution)/shard_map/slice | solution.py:458
  (4 shorter events, 0.0 us)
Async XLA Ops:
  6.8 7.4 %collective-permute-start = (f32[8,32,128]{2,1,0:T(8,128)S(1)}, f32[8,32,128]{2,1,0:T(8,128)S(1)}, u32[]{:S(2)}, u32[]{:S(2)}) collective-permute-start(f32[8,32,128]{2,1,0:T(8,128)S(1)} %get-tuple-element.16), channel_id=1, source_target_pairs={{0,15},{1,2},{2,1},{3,4},{4,3},{5,6},{6,5},{7,8},{8,7},{9,10},{10,... | collective-permute-start | bytes 393224 | tf_op jit(solution)/shard_map/ppermute | solution.py:426
  11.4 2.8 %collective-permute-start.1 = (f32[8,32,128]{2,1,0:T(8,128)S(1)}, f32[8,32,128]{2,1,0:T(8,128)S(1)}, u32[]{:S(2)}, u32[]{:S(2)}) collective-permute-start(f32[8,32,128]{2,1,0:T(8,128)S(1)} %get-tuple-element.17), channel_id=1, source_target_pairs={{0,1},{1,0},{2,3},{3,2},{4,5},{5,4},{6,7},{7,6},{8,9},{9,8},{10,11... | collective-permute-start | bytes 393224 | tf_op jit(solution)/shard_map/ppermute | solution.py:427
  19.2 1.2 %collective-permute-start.2 = (f32[8,128]{1,0:T(8,128)S(1)}, f32[8,128]{1,0:T(8,128)S(1)}, u32[]{:S(2)}, u32[]{:S(2)}) collective-permute-start(f32[8,128]{1,0:T(8,128)S(1)} %get-tuple-element.24), channel_id=1, source_target_pairs={{0,1},{1,0},{2,3},{3,2},{4,5},{5,4},{6,7},{7,6},{8,9},{9,8},{10,11... | collective-permute-start | bytes 12296 | tf_op jit(solution)/shard_map/ppermute | solution.py:384
  20.4 3.0 %collective-permute-start.3 = (f32[8,128]{1,0:T(8,128)S(1)}, f32[8,128]{1,0:T(8,128)S(1)}, u32[]{:S(2)}, u32[]{:S(2)}) collective-permute-start(f32[8,128]{1,0:T(8,128)S(1)} %max.12), channel_id=1, source_target_pairs={{0,3},{1,2},{2,1},{3,0},{4,7},{5,6},{6,5},{7,4},{8,11},{9,10},{10,... | collective-permute-start | bytes 12296 | tf_op jit(solution)/shard_map/ppermute | solution.py:384
  23.5 3.0 %collective-permute-start.4 = (f32[8,128]{1,0:T(8,128)S(1)}, f32[8,128]{1,0:T(8,128)S(1)}, u32[]{:S(2)}, u32[]{:S(2)}) collective-permute-start(f32[8,128]{1,0:T(8,128)S(1)} %max.13), channel_id=1, source_target_pairs={{0,5},{1,4},{2,7},{3,6},{4,1},{5,0},{6,3},{7,2},{8,13},{9,12},{10,... | collective-permute-start | bytes 12296 | tf_op jit(solution)/shard_map/ppermute | solution.py:384
  26.5 3.9 %collective-permute-start.5 = (f32[8,128]{1,0:T(8,128)S(1)}, f32[8,128]{1,0:T(8,128)S(1)}, u32[]{:S(2)}, u32[]{:S(2)}) collective-permute-start(f32[8,128]{1,0:T(8,128)S(1)} %max.14), channel_id=1, source_target_pairs={{0,9},{1,8},{2,11},{3,10},{4,13},{5,12},{6,15},{7,14},{8,1},{9,0},... | collective-permute-start | bytes 12296 | tf_op jit(solution)/shard_map/ppermute | solution.py:384

commit v5 on v4

--- a/solution.py
+++ b/solution.py
@@ -10,7 +10,8 @@
 CX = 2
 NY = 32
 NZ = 128
-ROWS = CX * NY
+PAIRS = CX * NY // 2
+WIDE = 2 * NZ
 BLOCK = 256
 LANES = 128
 UNROLL = 8
@@ -54,7 +55,7 @@
             jnp.concatenate(
                 [
                     jnp.where(line == (nodes + z).astype(bf16), one, zero)
-                    for z in range(0, NZ, 16)
+                    for z in range(0, WIDE, 16)
                 ],
                 axis=0,
             )
@@ -74,18 +75,18 @@
         jnp.where(slot < count, first_half, 0), jnp.where(slot + LANES < count, second_half, 0)
     )
     live = number * BLOCK < count
-    first = jnp.min(first_half, axis=1, keepdims=True) >> 7
-    last = jnp.max(reached, axis=1, keepdims=True) >> 7
+    first = jnp.min(first_half, axis=1, keepdims=True) >> 8
+    last = jnp.max(reached, axis=1, keepdims=True) >> 8
     low = jnp.where(live, first + number, 2 * LANES)
     high = jnp.where(live, last + number, -1)
     inside = (low <= lane) & (lane <= high)
     place = lane[:1]
     block = jnp.max(jnp.where(inside, number, -1), axis=0, keepdims=True)
     valid = block >= 0
-    row = place - block
+    pair = place - block
     plan_ref[0:1, :] = jnp.where(valid, block, 0)
-    plan_ref[1:2, :] = jnp.where(valid, row + (row >> 5), 0)
-    plan_ref[2:3, :] = jnp.where(valid, row, ROWS) * NZ
+    plan_ref[1:2, :] = jnp.where(valid, 2 * pair + (pair >> 4), 0)
+    plan_ref[2:3, :] = jnp.where(valid, pair, PAIRS) * WIDE
     plan_ref[3:4, :] = jnp.max(high, axis=0, keepdims=True) + 1
     plan_ref[4:5, :] = jnp.broadcast_to(count, (1, LANES))
     plan_ref[5:8, :] = jnp.zeros((3, LANES), jnp.int32)
@@ -164,11 +165,16 @@
             )
             found.append((listed_ref[1, v], both[:SPREAD] + both[SPREAD:]))
         for base, part in found:
-            here = pl.ds(pl.multiple_of(base * 8, 8), 16)
-            above = pl.ds(pl.multiple_of(base * 8, 8) + (NY + 1) * 8, 16)
+            here = pl.ds(pl.multiple_of(base * 8, 8), 24)
+            above = pl.ds(pl.multiple_of(base * 8, 8) + (NY + 1) * 8, 24)
             lower, upper = acc_ref[here, :], acc_ref[above, :]
-            acc_ref[here, :] = lower + part[:16]
-            acc_ref[above, :] = upper + part[16:]
+            first, second = part[:, :NZ], part[:, NZ:]
+            acc_ref[here, :] = lower + jnp.concatenate(
+                [first[0:8], first[8:16] + second[0:8], second[8:16]], axis=0
+            )
+            acc_ref[above, :] = upper + jnp.concatenate(
+                [first[16:24], first[24:32] + second[16:24], second[24:32]], axis=0
+            )
         return carry
 
     lax.fori_loop(0, (total + GIVEN - 1) // GIVEN, visit, 0)
@@ -301,7 +307,7 @@
         def split_row(j, carry):
             at = pl.ds(pl.multiple_of((l * NY + j) * TABLE, TABLE), TABLE)
             high, low = split_pair(tab_ref[at, :])
-            pair_ref[pl.ds(l * (NY + 1) + j, 1)] = jnp.concatenate([high, low], axis=1)[None]
+            pair_ref[pl.ds(l * (NY + 1) + j, 1)] = jnp.concatenate([high, low], axis=0)[None]
             return carry
 
         lax.fori_loop(0, NY, split_row, 0, unroll=8)
@@ -319,13 +325,15 @@
             block = listed_ref[0, v]
             base = listed_ref[1, v]
             hot = hot_ref[pl.ds(v, 1)][0]
-            rows = [pair_ref[base + ahead] for ahead in (0, 1, NY + 1, NY + 2)]
-            value = jnp.dot(
-                jnp.concatenate(rows, axis=0),
-                jnp.concatenate([hot, hot], axis=0),
-                preferred_element_type=f32,
-            )
-            corners = [value[8 * k : 8 * k + 8] for k in range(8)]
+            rows = []
+            for a in range(2):
+                three = [pair_ref[base + a * (NY + 1) + k] for k in range(3)]
+                rows += [jnp.concatenate(three[b : b + 2], axis=1) for b in range(2)]
+            both = jnp.dot(jnp.concatenate(rows, axis=0), hot, preferred_element_type=f32)
+            corners = []
+            for k in range(4):
+                four = both[2 * TABLE * k : 2 * TABLE * (k + 1)]
+                corners += [four[0:8] + four[16:24], four[8:16] + four[24:32]]
             frac = frac_ref[:, pl.ds(pl.multiple_of(block * BLOCK, BLOCK), BLOCK)]
             for d in (2, 1, 0):
                 share = frac[d : d + 1, :]
@@ -405,7 +413,7 @@
             pltpu.VMEM((8, LANES), jnp.int32),
             pltpu.VMEM(frac.shape, f32),
             pltpu.VMEM(velocity.shape, f32),
-            pltpu.VMEM((blocks + ROWS, NZ, BLOCK), bf16),
+            pltpu.VMEM((blocks + PAIRS, WIDE, BLOCK), bf16),
         ),
         in_specs=[smem] + [hbm] * 4,
         out_specs=(vmem,) * 7,
@@ -436,7 +444,7 @@
         scratch_shapes=[
             pltpu.SMEM((8, LANES), jnp.int32),
             pltpu.VMEM(((CX + 1) * NY * TABLE, NZ), f32),
-            pltpu.VMEM(((CX + 1) * (NY + 1), TABLE, 2 * NZ), bf16),
+            pltpu.VMEM(((CX + 1) * (NY + 1), 2 * TABLE, NZ), bf16),
             pltpu.SemaphoreType.DMA,
         ],
         compiler_params=pltpu.CompilerParams(vmem_limit_bytes=32 * 1024 * 1024),

time: 31.1 us -> 31.3 us (level)
  the two profiles are of different devices: /device:TPU:0 before, /device:TPU:3 now
where the time goes in v5:
time: 31.3 us; the launch traced here: 31.1 us
  starting transfers between devices  10.2 us (33%)
  waiting for transfers between devices  9.26 us (30%)
  Pallas kernels  9.2 us (29%)
  between operations  1.96 us (6%)
  local copies, waits for them, and re-layouts  0.52 us (2%)
    ppermute x4, waiting for transfers between devices, largest(): value = jnp.maximum(value, lax.ppermute(value, axis, pairs))  8.93 us
    ppermute x4, starting transfers between devices, largest(): value = jnp.maximum(value, lax.ppermute(value, axis, pairs))  5.43 us
    pallas_call x1, Pallas kernels, body(): pl.pallas_call(spread_kernel, out_shape=(pltpu.VMEM((4 * CX, NY, NZ), f32...  4.83 us
    pallas_call x1, Pallas kernels, body(): pl.pallas_call(collect_kernel, out_shape=(jax.ShapeDtypeStruct((blocks, 8...  3.37 us
    ppermute x1, starting transfers between devices, body(): near_new = lax.ppermute(near, 'gx', near_pairs)  2.87 us
    ppermute x1, starting transfers between devices, body(): far_new = lax.ppermute(far, 'gx', far_pairs)  1.86 us
    pallas_call x1, Pallas kernels, body(): pl.pallas_call(finish_kernel, out_shape=(jax.ShapeDtypeStruct(frac.shape,...  1 us
  transfers between devices with their start and end apart: 6, of which 5 were waited for; matrix products, arithmetic and copies ran while one was open for 0% of the time, Pallas kernels for 3%

profile of v5, /device:TPU:3, one launch (start us, length us, event | category | flops | bytes accessed | tf_op | source)
XLA Modules:
  0.0 31.1 jit_solution(12859014618263891065)
XLA Ops:
  1.3 4.8 %spread.1 = (f32[8,32,128]{2,1,0:T(8,128)S(1)}, f32[8,32,128]{2,1,0:T(8,128)S(1)}, f32[12,32,128]{2,1,0:T(8,128)S(1)}, s32[8,128]{1,0:T(8,128)S(1)}, f32[3,16384...) custom-call(s32[1]{0:T(128)S(6)} %copy.9.count_ref, f32[3,16384]{1,0:T(4,128)} %frac_hbm.1, ...), custom_call_target="tpu_custom_call" | custom-call | tf_op jit(solution)/shard_map/spread/pallas_call | solution.py:407
  6.1 1.9 %collective-permute-start = (f32[8,32,128]{2,1,0:T(8,128)S(1)}, f32[8,32,128]{2,1,0:T(8,128)S(1)}, u32[]{:S(2)}, u32[]{:S(2)}) collective-permute-start(f32[8,32,128]{2,1,0:T(8,128)S(1)} %get-tuple-element.16), channel_id=1, source_target_pairs={{0,15},{1,2},{2,1},{3,4},{4,3},{5,6},{6,5},{7,8},{8,7},{9,10},{10,... | collective-permute-start | bytes 393224 | tf_op jit(solution)/shard_map/ppermute | solution.py:434
  8.0 2.9 %collective-permute-start.1 = (f32[8,32,128]{2,1,0:T(8,128)S(1)}, f32[8,32,128]{2,1,0:T(8,128)S(1)}, u32[]{:S(2)}, u32[]{:S(2)}) collective-permute-start(f32[8,32,128]{2,1,0:T(8,128)S(1)} %get-tuple-element.17), channel_id=1, source_target_pairs={{0,1},{1,0},{2,3},{3,2},{4,5},{5,4},{6,7},{7,6},{8,9},{9,8},{10,11... | collective-permute-start | bytes 393224 | tf_op jit(solution)/shard_map/ppermute | solution.py:435
  11.5 0.0 collective-permute-done.far_new_ref
  11.5 0.3 %collective-permute-done.1.near_new_ref = f32[8,32,128]{2,1,0:T(8,128)S(1)} collective-permute-done((f32[8,32,128]{2,1,0:T(8,128)S(1)}, f32[8,32,128]{2,1,0:T(8,128)S(1)}, u32[]{:S(2)}, u32[]{:S(2)}) %collective-permute-start.1) | collective-permute-done | bytes 131104 | tf_op jit(solution)/shard_map/ppermute | solution.py:435
  11.8 3.4 %collect.1 = (f32[64,8,256]{2,1,0:T(8,128)S(1)}, f32[8,128]{1,0:T(8,128)S(1)}) custom-call(f32[1]{0:T(128)S(6)} %copy.10.step_ref, s32[8,128]{1,0:T(8,128)S(1)} %get-tuple-element.14.plan_ref, f32[12,32,128]{2,1,0:T(8,128)S(1)} %get-tuple-element.15.layers_ref, f32[8,32,128]{2,1,0:T(8,128)S(1)} %collective-permute-done.far_new_ref, ...), custom_call_target="tpu_custom_call" | custom-call | tf_op jit(solution)/shard_map/collect/pallas_call | solution.py:436
  15.2 4.5 %collective-permute-start.2 = (f32[8,128]{1,0:T(8,128)S(1)}, f32[8,128]{1,0:T(8,128)S(1)}, u32[]{:S(2)}, u32[]{:S(2)}) collective-permute-start(f32[8,128]{1,0:T(8,128)S(1)} %get-tuple-element.24), channel_id=1, source_target_pairs={{0,1},{1,0},{2,3},{3,2},{4,5},{5,4},{6,7},{7,6},{8,9},{9,8},{10,11... | collective-permute-start | bytes 12296 | tf_op jit(solution)/shard_map/ppermute | solution.py:392
  19.8 0.8 %collective-permute-done.2 = f32[8,128]{1,0:T(8,128)S(1)} collective-permute-done((f32[8,128]{1,0:T(8,128)S(1)}, f32[8,128]{1,0:T(8,128)S(1)}, u32[]{:S(2)}, u32[]{:S(2)}) %collective-permute-start.2) | collective-permute-done | bytes 4128 | tf_op jit(solution)/shard_map/ppermute | solution.py:392
  20.6 0.0 collective-permute-start.3
  20.6 3.0 %collective-permute-done.3 = f32[8,128]{1,0:T(8,128)S(1)} collective-permute-done((f32[8,128]{1,0:T(8,128)S(1)}, f32[8,128]{1,0:T(8,128)S(1)}, u32[]{:S(2)}, u32[]{:S(2)}) %collective-permute-start.3) | collective-permute-done | bytes 4128 | tf_op jit(solution)/shard_map/ppermute | solution.py:392
  23.6 0.0 collective-permute-start.4
  23.6 3.0 %collective-permute-done.4 = f32[8,128]{1,0:T(8,128)S(1)} collective-permute-done((f32[8,128]{1,0:T(8,128)S(1)}, f32[8,128]{1,0:T(8,128)S(1)}, u32[]{:S(2)}, u32[]{:S(2)}) %collective-permute-start.4) | collective-permute-done | bytes 4128 | tf_op jit(solution)/shard_map/ppermute | solution.py:392
  26.7 0.9 %collective-permute-start.5 = (f32[8,128]{1,0:T(8,128)S(1)}, f32[8,128]{1,0:T(8,128)S(1)}, u32[]{:S(2)}, u32[]{:S(2)}) collective-permute-start(f32[8,128]{1,0:T(8,128)S(1)} %max.14), channel_id=1, source_target_pairs={{0,9},{1,8},{2,11},{3,10},{4,13},{5,12},{6,15},{7,14},{8,1},{9,0},... | collective-permute-start | bytes 12296 | tf_op jit(solution)/shard_map/ppermute | solution.py:392
  27.5 1.0 %finish.1 = (f32[3,16384]{1,0:T(4,128)}, f32[3,16384]{1,0:T(4,128)}) custom-call(s32[8,128]{1,0:T(8,128)S(1)} %get-tuple-element.14.plan_ref, f32[64,8,256]{2,1,0:T(8,128)S(1)} %get-tuple-element.21.moved_ref, f32[3,16384]{1,0:T(4,128)S(1)} %get-tuple-element.18.frac_ref), custom_call_target="tpu_custom_call" | custom-call | bytes 8000000 | tf_op jit(solution)/shard_map/finish/pallas_call | solution.py:453
  28.5 2.0 %collective-permute-done.5 = f32[8,128]{1,0:T(8,128)S(1)} collective-permute-done((f32[8,128]{1,0:T(8,128)S(1)}, f32[8,128]{1,0:T(8,128)S(1)}, u32[]{:S(2)}, u32[]{:S(2)}) %collective-permute-start.5) | collective-permute-done | bytes 4128 | tf_op jit(solution)/shard_map/ppermute | solution.py:392
  30.6 0.5 %slice.3 = f32[1,1]{1,0:T(1,128)} slice(f32[8,128]{1,0:T(8,128)S(1)} %add_divide_fusion), slice={[0:1], [0:1]} | slice | bytes 8 | tf_op jit(solution)/shard_map/slice | solution.py:466
  (4 shorter events, 0.0 us)
Async XLA Ops:
  6.1 5.4 %collective-permute-start = (f32[8,32,128]{2,1,0:T(8,128)S(1)}, f32[8,32,128]{2,1,0:T(8,128)S(1)}, u32[]{:S(2)}, u32[]{:S(2)}) collective-permute-start(f32[8,32,128]{2,1,0:T(8,128)S(1)} %get-tuple-element.16), channel_id=1, source_target_pairs={{0,15},{1,2},{2,1},{3,4},{4,3},{5,6},{6,5},{7,8},{8,7},{9,10},{10,... | collective-permute-start | bytes 393224 | tf_op jit(solution)/shard_map/ppermute | solution.py:434
  8.0 3.9 %collective-permute-start.1 = (f32[8,32,128]{2,1,0:T(8,128)S(1)}, f32[8,32,128]{2,1,0:T(8,128)S(1)}, u32[]{:S(2)}, u32[]{:S(2)}) collective-permute-start(f32[8,32,128]{2,1,0:T(8,128)S(1)} %get-tuple-element.17), channel_id=1, source_target_pairs={{0,1},{1,0},{2,3},{3,2},{4,5},{5,4},{6,7},{7,6},{8,9},{9,8},{10,11... | collective-permute-start | bytes 393224 | tf_op jit(solution)/shard_map/ppermute | solution.py:435
  15.2 5.4 %collective-permute-start.2 = (f32[8,128]{1,0:T(8,128)S(1)}, f32[8,128]{1,0:T(8,128)S(1)}, u32[]{:S(2)}, u32[]{:S(2)}) collective-permute-start(f32[8,128]{1,0:T(8,128)S(1)} %get-tuple-element.24), channel_id=1, source_target_pairs={{0,1},{1,0},{2,3},{3,2},{4,5},{5,4},{6,7},{7,6},{8,9},{9,8},{10,11... | collective-permute-start | bytes 12296 | tf_op jit(solution)/shard_map/ppermute | solution.py:392
  20.6 3.0 %collective-permute-start.3 = (f32[8,128]{1,0:T(8,128)S(1)}, f32[8,128]{1,0:T(8,128)S(1)}, u32[]{:S(2)}, u32[]{:S(2)}) collective-permute-start(f32[8,128]{1,0:T(8,128)S(1)} %max.12), channel_id=1, source_target_pairs={{0,3},{1,2},{2,1},{3,0},{4,7},{5,6},{6,5},{7,4},{8,11},{9,10},{10,... | collective-permute-start | bytes 12296 | tf_op jit(solution)/shard_map/ppermute | solution.py:392
  23.6 3.0 %collective-permute-start.4 = (f32[8,128]{1,0:T(8,128)S(1)}, f32[8,128]{1,0:T(8,128)S(1)}, u32[]{:S(2)}, u32[]{:S(2)}) collective-permute-start(f32[8,128]{1,0:T(8,128)S(1)} %max.13), channel_id=1, source_target_pairs={{0,5},{1,4},{2,7},{3,6},{4,1},{5,0},{6,3},{7,2},{8,13},{9,12},{10,... | collective-permute-start | bytes 12296 | tf_op jit(solution)/shard_map/ppermute | solution.py:392
  26.7 3.9 %collective-permute-start.5 = (f32[8,128]{1,0:T(8,128)S(1)}, f32[8,128]{1,0:T(8,128)S(1)}, u32[]{:S(2)}, u32[]{:S(2)}) collective-permute-start(f32[8,128]{1,0:T(8,128)S(1)} %max.14), channel_id=1, source_target_pairs={{0,9},{1,8},{2,11},{3,10},{4,13},{5,12},{6,15},{7,14},{8,1},{9,0},... | collective-permute-start | bytes 12296 | tf_op jit(solution)/shard_map/ppermute | solution.py:392

commit v6 on v5

--- a/solution.py
+++ b/solution.py
@@ -51,15 +51,11 @@
     halves = []
     for h in range(2):
         line = jnp.broadcast_to(rel[h : h + 1, :].astype(f32), tall).astype(bf16)
-        halves.append(
-            jnp.concatenate(
-                [
-                    jnp.where(line == (nodes + z).astype(bf16), one, zero)
-                    for z in range(0, WIDE, 16)
-                ],
-                axis=0,
-            )
-        )
+        parts = []
+        for z in range(0, WIDE, 16):
+            apart = line - (nodes + z).astype(bf16)
+            parts.append(jnp.maximum(one - apart * apart, zero))
+        halves.append(jnp.concatenate(parts, axis=0))
     return jnp.concatenate(halves, axis=1)
 
 

time: 31.3 us -> 31 us (level)
  the two profiles are of different devices: /device:TPU:3 before, /device:TPU:0 now
where the time goes in v6:
time: 31 us; the launch traced here: 30.6 us
  starting transfers between devices  12.2 us (39%)
  Pallas kernels  9.22 us (30%)
  waiting for transfers between devices  6.63 us (21%)
  between operations  1.95 us (6%)
  local copies, waits for them, and re-layouts  0.52 us (2%)
    ppermute x4, starting transfers between devices, largest(): value = jnp.maximum(value, lax.ppermute(value, axis, pairs))  6.71 us
    ppermute x1, starting transfers between devices, body(): far_new = lax.ppermute(far, 'gx', far_pairs)  5.51 us
    pallas_call x1, Pallas kernels, body(): pl.pallas_call(spread_kernel, out_shape=(pltpu.VMEM((4 * CX, NY, NZ), f32...  4.84 us
    ppermute x4, waiting for transfers between devices, largest(): value = jnp.maximum(value, lax.ppermute(value, axis, pairs))  4.53 us
    pallas_call x1, Pallas kernels, body(): pl.pallas_call(collect_kernel, out_shape=(jax.ShapeDtypeStruct((blocks, 8...  3.37 us
    ppermute x1, waiting for transfers between devices, body(): far_new = lax.ppermute(far, 'gx', far_pairs)  2.1 us
    pallas_call x1, Pallas kernels, body(): pl.pallas_call(finish_kernel, out_shape=(jax.ShapeDtypeStruct(frac.shape,...  1 us
  transfers between devices with their start and end apart: 6, of which 5 were waited for; matrix products, arithmetic and copies ran while one was open for 0% of the time, Pallas kernels for 3%

profile of v6, /device:TPU:0, one launch (start us, length us, event | category | flops | bytes accessed | tf_op | source)
XLA Modules:
  0.0 30.6 jit_solution(15524549091713277179)
XLA Ops:
  1.3 4.8 %spread.1 = (f32[8,32,128]{2,1,0:T(8,128)S(1)}, f32[8,32,128]{2,1,0:T(8,128)S(1)}, f32[12,32,128]{2,1,0:T(8,128)S(1)}, s32[8,128]{1,0:T(8,128)S(1)}, f32[3,16384...) custom-call(s32[1]{0:T(128)S(6)} %copy.9.count_ref, f32[3,16384]{1,0:T(4,128)} %frac_hbm.1, ...), custom_call_target="tpu_custom_call" | custom-call | tf_op jit(solution)/shard_map/spread/pallas_call | solution.py:403
  6.1 5.5 %collective-permute-start = (f32[8,32,128]{2,1,0:T(8,128)S(1)}, f32[8,32,128]{2,1,0:T(8,128)S(1)}, u32[]{:S(2)}, u32[]{:S(2)}) collective-permute-start(f32[8,32,128]{2,1,0:T(8,128)S(1)} %get-tuple-element.16), channel_id=1, source_target_pairs={{0,15},{1,2},{2,1},{3,4},{4,3},{5,6},{6,5},{7,8},{8,7},{9,10},{10,... | collective-permute-start | bytes 393224 | tf_op jit(solution)/shard_map/ppermute | solution.py:430
  11.6 0.0 collective-permute-start.1
  12.3 2.1 %collective-permute-done.far_new_ref = f32[8,32,128]{2,1,0:T(8,128)S(1)} collective-permute-done((f32[8,32,128]{2,1,0:T(8,128)S(1)}, f32[8,32,128]{2,1,0:T(8,128)S(1)}, u32[]{:S(2)}, u32[]{:S(2)}) %collective-permute-start) | collective-permute-done | bytes 131104 | tf_op jit(solution)/shard_map/ppermute | solution.py:430
  14.4 0.0 collective-permute-done.1.near_new_ref
  14.4 3.4 %collect.1 = (f32[64,8,256]{2,1,0:T(8,128)S(1)}, f32[8,128]{1,0:T(8,128)S(1)}) custom-call(f32[1]{0:T(128)S(6)} %copy.10.step_ref, s32[8,128]{1,0:T(8,128)S(1)} %get-tuple-element.14.plan_ref, f32[12,32,128]{2,1,0:T(8,128)S(1)} %get-tuple-element.15.layers_ref, f32[8,32,128]{2,1,0:T(8,128)S(1)} %collective-permute-done.far_new_ref, ...), custom_call_target="tpu_custom_call" | custom-call | tf_op jit(solution)/shard_map/collect/pallas_call | solution.py:432
  17.8 1.4 %collective-permute-start.2 = (f32[8,128]{1,0:T(8,128)S(1)}, f32[8,128]{1,0:T(8,128)S(1)}, u32[]{:S(2)}, u32[]{:S(2)}) collective-permute-start(f32[8,128]{1,0:T(8,128)S(1)} %get-tuple-element.24), channel_id=1, source_target_pairs={{0,1},{1,0},{2,3},{3,2},{4,5},{5,4},{6,7},{7,6},{8,9},{9,8},{10,11... | collective-permute-start | bytes 12296 | tf_op jit(solution)/shard_map/ppermute | solution.py:388
  19.2 0.8 %collective-permute-done.2 = f32[8,128]{1,0:T(8,128)S(1)} collective-permute-done((f32[8,128]{1,0:T(8,128)S(1)}, f32[8,128]{1,0:T(8,128)S(1)}, u32[]{:S(2)}, u32[]{:S(2)}) %collective-permute-start.2) | collective-permute-done | bytes 4128 | tf_op jit(solution)/shard_map/ppermute | solution.py:388
  20.0 1.7 %collective-permute-start.3 = (f32[8,128]{1,0:T(8,128)S(1)}, f32[8,128]{1,0:T(8,128)S(1)}, u32[]{:S(2)}, u32[]{:S(2)}) collective-permute-start(f32[8,128]{1,0:T(8,128)S(1)} %max.12), channel_id=1, source_target_pairs={{0,3},{1,2},{2,1},{3,0},{4,7},{5,6},{6,5},{7,4},{8,11},{9,10},{10,... | collective-permute-start | bytes 12296 | tf_op jit(solution)/shard_map/ppermute | solution.py:388
  21.7 1.3 %collective-permute-done.3 = f32[8,128]{1,0:T(8,128)S(1)} collective-permute-done((f32[8,128]{1,0:T(8,128)S(1)}, f32[8,128]{1,0:T(8,128)S(1)}, u32[]{:S(2)}, u32[]{:S(2)}) %collective-permute-start.3) | collective-permute-done | bytes 4128 | tf_op jit(solution)/shard_map/ppermute | solution.py:388
  23.1 1.4 %collective-permute-start.4 = (f32[8,128]{1,0:T(8,128)S(1)}, f32[8,128]{1,0:T(8,128)S(1)}, u32[]{:S(2)}, u32[]{:S(2)}) collective-permute-start(f32[8,128]{1,0:T(8,128)S(1)} %max.13), channel_id=1, source_target_pairs={{0,5},{1,4},{2,7},{3,6},{4,1},{5,0},{6,3},{7,2},{8,13},{9,12},{10,... | collective-permute-start | bytes 12296 | tf_op jit(solution)/shard_map/ppermute | solution.py:388
  24.5 1.6 %collective-permute-done.4 = f32[8,128]{1,0:T(8,128)S(1)} collective-permute-done((f32[8,128]{1,0:T(8,128)S(1)}, f32[8,128]{1,0:T(8,128)S(1)}, u32[]{:S(2)}, u32[]{:S(2)}) %collective-permute-start.4) | collective-permute-done | bytes 4128 | tf_op jit(solution)/shard_map/ppermute | solution.py:388
  26.1 2.2 %collective-permute-start.5 = (f32[8,128]{1,0:T(8,128)S(1)}, f32[8,128]{1,0:T(8,128)S(1)}, u32[]{:S(2)}, u32[]{:S(2)}) collective-permute-start(f32[8,128]{1,0:T(8,128)S(1)} %max.14), channel_id=1, source_target_pairs={{0,9},{1,8},{2,11},{3,10},{4,13},{5,12},{6,15},{7,14},{8,1},{9,0},... | collective-permute-start | bytes 12296 | tf_op jit(solution)/shard_map/ppermute | solution.py:388
  28.3 1.0 %finish.1 = (f32[3,16384]{1,0:T(4,128)}, f32[3,16384]{1,0:T(4,128)}) custom-call(s32[8,128]{1,0:T(8,128)S(1)} %get-tuple-element.14.plan_ref, f32[64,8,256]{2,1,0:T(8,128)S(1)} %get-tuple-element.21.moved_ref, f32[3,16384]{1,0:T(4,128)S(1)} %get-tuple-element.18.frac_ref), custom_call_target="tpu_custom_call" | custom-call | bytes 8000000 | tf_op jit(solution)/shard_map/finish/pallas_call | solution.py:449
  29.3 0.8 %collective-permute-done.5 = f32[8,128]{1,0:T(8,128)S(1)} collective-permute-done((f32[8,128]{1,0:T(8,128)S(1)}, f32[8,128]{1,0:T(8,128)S(1)}, u32[]{:S(2)}, u32[]{:S(2)}) %collective-permute-start.5) | collective-permute-done | bytes 4128 | tf_op jit(solution)/shard_map/ppermute | solution.py:388
  30.0 0.5 %slice.3 = f32[1,1]{1,0:T(1,128)} slice(f32[8,128]{1,0:T(8,128)S(1)} %add_divide_fusion), slice={[0:1], [0:1]} | slice | bytes 8 | tf_op jit(solution)/shard_map/slice | solution.py:462
  (4 shorter events, 0.0 us)
Async XLA Ops:
  6.1 8.3 %collective-permute-start = (f32[8,32,128]{2,1,0:T(8,128)S(1)}, f32[8,32,128]{2,1,0:T(8,128)S(1)}, u32[]{:S(2)}, u32[]{:S(2)}) collective-permute-start(f32[8,32,128]{2,1,0:T(8,128)S(1)} %get-tuple-element.16), channel_id=1, source_target_pairs={{0,15},{1,2},{2,1},{3,4},{4,3},{5,6},{6,5},{7,8},{8,7},{9,10},{10,... | collective-permute-start | bytes 393224 | tf_op jit(solution)/shard_map/ppermute | solution.py:430
  11.6 2.8 %collective-permute-start.1 = (f32[8,32,128]{2,1,0:T(8,128)S(1)}, f32[8,32,128]{2,1,0:T(8,128)S(1)}, u32[]{:S(2)}, u32[]{:S(2)}) collective-permute-start(f32[8,32,128]{2,1,0:T(8,128)S(1)} %get-tuple-element.17), channel_id=1, source_target_pairs={{0,1},{1,0},{2,3},{3,2},{4,5},{5,4},{6,7},{7,6},{8,9},{9,8},{10,11... | collective-permute-start | bytes 393224 | tf_op jit(solution)/shard_map/ppermute | solution.py:431
  17.8 2.2 %collective-permute-start.2 = (f32[8,128]{1,0:T(8,128)S(1)}, f32[8,128]{1,0:T(8,128)S(1)}, u32[]{:S(2)}, u32[]{:S(2)}) collective-permute-start(f32[8,128]{1,0:T(8,128)S(1)} %get-tuple-element.24), channel_id=1, source_target_pairs={{0,1},{1,0},{2,3},{3,2},{4,5},{5,4},{6,7},{7,6},{8,9},{9,8},{10,11... | collective-permute-start | bytes 12296 | tf_op jit(solution)/shard_map/ppermute | solution.py:388
  20.0 3.1 %collective-permute-start.3 = (f32[8,128]{1,0:T(8,128)S(1)}, f32[8,128]{1,0:T(8,128)S(1)}, u32[]{:S(2)}, u32[]{:S(2)}) collective-permute-start(f32[8,128]{1,0:T(8,128)S(1)} %max.12), channel_id=1, source_target_pairs={{0,3},{1,2},{2,1},{3,0},{4,7},{5,6},{6,5},{7,4},{8,11},{9,10},{10,... | collective-permute-start | bytes 12296 | tf_op jit(solution)/shard_map/ppermute | solution.py:388
  23.1 3.0 %collective-permute-start.4 = (f32[8,128]{1,0:T(8,128)S(1)}, f32[8,128]{1,0:T(8,128)S(1)}, u32[]{:S(2)}, u32[]{:S(2)}) collective-permute-start(f32[8,128]{1,0:T(8,128)S(1)} %max.13), channel_id=1, source_target_pairs={{0,5},{1,4},{2,7},{3,6},{4,1},{5,0},{6,3},{7,2},{8,13},{9,12},{10,... | collective-permute-start | bytes 12296 | tf_op jit(solution)/shard_map/ppermute | solution.py:388
  26.1 3.9 %collective-permute-start.5 = (f32[8,128]{1,0:T(8,128)S(1)}, f32[8,128]{1,0:T(8,128)S(1)}, u32[]{:S(2)}, u32[]{:S(2)}) collective-permute-start(f32[8,128]{1,0:T(8,128)S(1)} %max.14), channel_id=1, source_target_pairs={{0,9},{1,8},{2,11},{3,10},{4,13},{5,12},{6,15},{7,14},{8,1},{9,0},... | collective-permute-start | bytes 12296 | tf_op jit(solution)/shard_map/ppermute | solution.py:388

commit v7 on v6

--- a/solution.py
+++ b/solution.py
@@ -17,6 +17,8 @@
 UNROLL = 8
 GIVEN = 32
 TAKEN = 32
+SLOTS = 8
+DELAY = 4
 SPREAD = 32
 TABLE = 16
 
@@ -146,31 +148,43 @@
     total = listed_ref[3, 0]
 
     def visit(group, carry):
-        found = []
-        for u in range(GIVEN):
-            v = group * GIVEN + u
-            block = listed_ref[0, v]
-            hot = one_hot(cells_ref, block, listed_ref[2, v])
-            hot_ref[pl.ds(v, 1)] = hot[None]
-            both = q_ref[pl.ds(block * 2, 2)]
-            both = lax.dot_general(
-                jnp.concatenate([both[0], both[1]], axis=1),
-                hot,
-                (((1,), (1,)), ((), ())),
-                preferred_element_type=f32,
-            )
-            found.append((listed_ref[1, v], both[:SPREAD] + both[SPREAD:]))
-        for base, part in found:
-            here = pl.ds(pl.multiple_of(base * 8, 8), 24)
-            above = pl.ds(pl.multiple_of(base * 8, 8) + (NY + 1) * 8, 24)
-            lower, upper = acc_ref[here, :], acc_ref[above, :]
-            first, second = part[:, :NZ], part[:, NZ:]
-            acc_ref[here, :] = lower + jnp.concatenate(
-                [first[0:8], first[8:16] + second[0:8], second[8:16]], axis=0
-            )
-            acc_ref[above, :] = upper + jnp.concatenate(
-                [first[16:24], first[24:32] + second[16:24], second[24:32]], axis=0
-            )
+        def run(*sums):
+            found = []
+
+            def take(u):
+                both = pltpu.matmul_pop(sums[u % SLOTS])
+                found.append((listed_ref[1, group * GIVEN + u], both[:SPREAD] + both[SPREAD:]))
+
+            for u in range(GIVEN):
+                v = group * GIVEN + u
+                block = listed_ref[0, v]
+                hot = one_hot(cells_ref, block, listed_ref[2, v])
+                hot_ref[pl.ds(v, 1)] = hot[None]
+                both = q_ref[pl.ds(block * 2, 2)]
+                unit, turn = u % 2, u // 2 % 2
+                pltpu.matmul_push_rhs(hot, turn, unit, transpose=True)
+                pltpu.matmul_acc_lhs(
+                    sums[u % SLOTS],
+                    jnp.concatenate([both[0], both[1]], axis=1),
+                    load_staged_rhs=turn,
+                )
+                if u >= DELAY:
+                    take(u - DELAY)
+            for u in range(GIVEN - DELAY, GIVEN):
+                take(u)
+            for base, part in found:
+                here = pl.ds(pl.multiple_of(base * 8, 8), 24)
+                above = pl.ds(pl.multiple_of(base * 8, 8) + (NY + 1) * 8, 24)
+                lower, upper = acc_ref[here, :], acc_ref[above, :]
+                first, second = part[:, :NZ], part[:, NZ:]
+                acc_ref[here, :] = lower + jnp.concatenate(
+                    [first[0:8], first[8:16] + second[0:8], second[8:16]], axis=0
+                )
+                acc_ref[above, :] = upper + jnp.concatenate(
+                    [first[16:24], first[24:32] + second[16:24], second[24:32]], axis=0
+                )
+
+        pl.run_scoped(run, *[pltpu.ACC(k % 2)((2 * SPREAD, WIDE), f32) for k in range(SLOTS)])
         return carry
 
     lax.fori_loop(0, (total + GIVEN - 1) // GIVEN, visit, 0)

time: 31 us -> 31.2 us (level)
  waiting for transfers between devices: 6.63 us -> 7.44 us
    ppermute x4, starting transfers between devices: 6.71 us -> 4.99 us  [largest(): value = jnp.maximum(value, lax.ppermute(value, axis, pairs))]
    ppermute x1, starting transfers between devices: 5.51 us -> 6.93 us  [body(): far_new = lax.ppermute(far, 'gx', far_pairs)]
    ppermute x4, waiting for transfers between devices: 4.53 us -> 5.43 us  [largest(): value = jnp.maximum(value, lax.ppermute(value, axis, pairs))]
where the time goes in v7:
time: 31.2 us; the launch traced here: 31 us
  starting transfers between devices  11.9 us (38%)
  Pallas kernels  9.15 us (29%)
  waiting for transfers between devices  7.44 us (24%)
  between operations  1.96 us (6%)
  local copies, waits for them, and re-layouts  0.52 us (2%)
    ppermute x1, starting transfers between devices, body(): far_new = lax.ppermute(far, 'gx', far_pairs)  6.93 us
    ppermute x4, waiting for transfers between devices, largest(): value = jnp.maximum(value, lax.ppermute(value, axis, pairs))  5.43 us
    ppermute x4, starting transfers between devices, largest(): value = jnp.maximum(value, lax.ppermute(value, axis, pairs))  4.99 us
    pallas_call x1, Pallas kernels, body(): pl.pallas_call(spread_kernel, out_shape=(pltpu.VMEM((4 * CX, NY, NZ), f32...  4.79 us
    pallas_call x1, Pallas kernels, body(): pl.pallas_call(collect_kernel, out_shape=(jax.ShapeDtypeStruct((blocks, 8...  3.36 us
    ppermute x1, waiting for transfers between devices, body(): far_new = lax.ppermute(far, 'gx', far_pairs)  2 us
    pallas_call x1, Pallas kernels, body(): pl.pallas_call(finish_kernel, out_shape=(jax.ShapeDtypeStruct(frac.shape,...  1 us
  transfers between devices with their start and end apart: 6, of which 5 were waited for; matrix products, arithmetic and copies ran while one was open for 0% of the time, Pallas kernels for 3%

profile of v7, /device:TPU:0, one launch (start us, length us, event | category | flops | bytes accessed | tf_op | source)
XLA Modules:
  0.0 31.0 jit_solution(2441486236843344031)
XLA Ops:
  1.3 4.8 %spread.1 = (f32[8,32,128]{2,1,0:T(8,128)S(1)}, f32[8,32,128]{2,1,0:T(8,128)S(1)}, f32[12,32,128]{2,1,0:T(8,128)S(1)}, s32[8,128]{1,0:T(8,128)S(1)}, f32[3,16384...) custom-call(s32[1]{0:T(128)S(6)} %copy.9.count_ref, f32[3,16384]{1,0:T(4,128)} %frac_hbm.1, ...), custom_call_target="tpu_custom_call" | custom-call | tf_op jit(solution)/shard_map/spread/pallas_call | solution.py:417
  6.1 6.9 %collective-permute-start = (f32[8,32,128]{2,1,0:T(8,128)S(1)}, f32[8,32,128]{2,1,0:T(8,128)S(1)}, u32[]{:S(2)}, u32[]{:S(2)}) collective-permute-start(f32[8,32,128]{2,1,0:T(8,128)S(1)} %get-tuple-element.16), channel_id=1, source_target_pairs={{0,15},{1,2},{2,1},{3,4},{4,3},{5,6},{6,5},{7,8},{8,7},{9,10},{10,... | collective-permute-start | bytes 393224 | tf_op jit(solution)/shard_map/ppermute | solution.py:444
  13.0 0.0 collective-permute-start.1
  13.7 2.0 %collective-permute-done.far_new_ref = f32[8,32,128]{2,1,0:T(8,128)S(1)} collective-permute-done((f32[8,32,128]{2,1,0:T(8,128)S(1)}, f32[8,32,128]{2,1,0:T(8,128)S(1)}, u32[]{:S(2)}, u32[]{:S(2)}) %collective-permute-start) | collective-permute-done | bytes 131104 | tf_op jit(solution)/shard_map/ppermute | solution.py:444
  15.7 0.0 collective-permute-done.1.near_new_ref
  15.7 3.4 %collect.1 = (f32[64,8,256]{2,1,0:T(8,128)S(1)}, f32[8,128]{1,0:T(8,128)S(1)}) custom-call(f32[1]{0:T(128)S(6)} %copy.10.step_ref, s32[8,128]{1,0:T(8,128)S(1)} %get-tuple-element.14.plan_ref, f32[12,32,128]{2,1,0:T(8,128)S(1)} %get-tuple-element.15.layers_ref, f32[8,32,128]{2,1,0:T(8,128)S(1)} %collective-permute-done.far_new_ref, ...), custom_call_target="tpu_custom_call" | custom-call | tf_op jit(solution)/shard_map/collect/pallas_call | solution.py:446
  19.0 0.1 collective-permute-start.2
  19.1 1.2 %collective-permute-done.2 = f32[8,128]{1,0:T(8,128)S(1)} collective-permute-done((f32[8,128]{1,0:T(8,128)S(1)}, f32[8,128]{1,0:T(8,128)S(1)}, u32[]{:S(2)}, u32[]{:S(2)}) %collective-permute-start.2) | collective-permute-done | bytes 4128 | tf_op jit(solution)/shard_map/ppermute | solution.py:402
  20.3 0.9 %collective-permute-start.3 = (f32[8,128]{1,0:T(8,128)S(1)}, f32[8,128]{1,0:T(8,128)S(1)}, u32[]{:S(2)}, u32[]{:S(2)}) collective-permute-start(f32[8,128]{1,0:T(8,128)S(1)} %max.12), channel_id=1, source_target_pairs={{0,3},{1,2},{2,1},{3,0},{4,7},{5,6},{6,5},{7,4},{8,11},{9,10},{10,... | collective-permute-start | bytes 12296 | tf_op jit(solution)/shard_map/ppermute | solution.py:402
  21.2 2.1 %collective-permute-done.3 = f32[8,128]{1,0:T(8,128)S(1)} collective-permute-done((f32[8,128]{1,0:T(8,128)S(1)}, f32[8,128]{1,0:T(8,128)S(1)}, u32[]{:S(2)}, u32[]{:S(2)}) %collective-permute-start.3) | collective-permute-done | bytes 4128 | tf_op jit(solution)/shard_map/ppermute | solution.py:402
  23.3 1.2 %collective-permute-start.4 = (f32[8,128]{1,0:T(8,128)S(1)}, f32[8,128]{1,0:T(8,128)S(1)}, u32[]{:S(2)}, u32[]{:S(2)}) collective-permute-start(f32[8,128]{1,0:T(8,128)S(1)} %max.13), channel_id=1, source_target_pairs={{0,5},{1,4},{2,7},{3,6},{4,1},{5,0},{6,3},{7,2},{8,13},{9,12},{10,... | collective-permute-start | bytes 12296 | tf_op jit(solution)/shard_map/ppermute | solution.py:402
  24.5 1.9 %collective-permute-done.4 = f32[8,128]{1,0:T(8,128)S(1)} collective-permute-done((f32[8,128]{1,0:T(8,128)S(1)}, f32[8,128]{1,0:T(8,128)S(1)}, u32[]{:S(2)}, u32[]{:S(2)}) %collective-permute-start.4) | collective-permute-done | bytes 4128 | tf_op jit(solution)/shard_map/ppermute | solution.py:402
  26.3 2.8 %collective-permute-start.5 = (f32[8,128]{1,0:T(8,128)S(1)}, f32[8,128]{1,0:T(8,128)S(1)}, u32[]{:S(2)}, u32[]{:S(2)}) collective-permute-start(f32[8,128]{1,0:T(8,128)S(1)} %max.14), channel_id=1, source_target_pairs={{0,9},{1,8},{2,11},{3,10},{4,13},{5,12},{6,15},{7,14},{8,1},{9,0},... | collective-permute-start | bytes 12296 | tf_op jit(solution)/shard_map/ppermute | solution.py:402
  29.1 1.0 %finish.1 = (f32[3,16384]{1,0:T(4,128)}, f32[3,16384]{1,0:T(4,128)}) custom-call(s32[8,128]{1,0:T(8,128)S(1)} %get-tuple-element.14.plan_ref, f32[64,8,256]{2,1,0:T(8,128)S(1)} %get-tuple-element.21.moved_ref, f32[3,16384]{1,0:T(4,128)S(1)} %get-tuple-element.18.frac_ref), custom_call_target="tpu_custom_call" | custom-call | bytes 8000000 | tf_op jit(solution)/shard_map/finish/pallas_call | solution.py:463
  30.2 0.3 %collective-permute-done.5 = f32[8,128]{1,0:T(8,128)S(1)} collective-permute-done((f32[8,128]{1,0:T(8,128)S(1)}, f32[8,128]{1,0:T(8,128)S(1)}, u32[]{:S(2)}, u32[]{:S(2)}) %collective-permute-start.5) | collective-permute-done | bytes 4128 | tf_op jit(solution)/shard_map/ppermute | solution.py:402
  30.5 0.5 %slice.3 = f32[1,1]{1,0:T(1,128)} slice(f32[8,128]{1,0:T(8,128)S(1)} %add_divide_fusion), slice={[0:1], [0:1]} | slice | bytes 8 | tf_op jit(solution)/shard_map/slice | solution.py:476
  (4 shorter events, 0.0 us)
Async XLA Ops:
  6.1 9.6 %collective-permute-start = (f32[8,32,128]{2,1,0:T(8,128)S(1)}, f32[8,32,128]{2,1,0:T(8,128)S(1)}, u32[]{:S(2)}, u32[]{:S(2)}) collective-permute-start(f32[8,32,128]{2,1,0:T(8,128)S(1)} %get-tuple-element.16), channel_id=1, source_target_pairs={{0,15},{1,2},{2,1},{3,4},{4,3},{5,6},{6,5},{7,8},{8,7},{9,10},{10,... | collective-permute-start | bytes 393224 | tf_op jit(solution)/shard_map/ppermute | solution.py:444
  13.0 2.7 %collective-permute-start.1 = (f32[8,32,128]{2,1,0:T(8,128)S(1)}, f32[8,32,128]{2,1,0:T(8,128)S(1)}, u32[]{:S(2)}, u32[]{:S(2)}) collective-permute-start(f32[8,32,128]{2,1,0:T(8,128)S(1)} %get-tuple-element.17), channel_id=1, source_target_pairs={{0,1},{1,0},{2,3},{3,2},{4,5},{5,4},{6,7},{7,6},{8,9},{9,8},{10,11... | collective-permute-start | bytes 393224 | tf_op jit(solution)/shard_map/ppermute | solution.py:445
  19.0 1.2 %collective-permute-start.2 = (f32[8,128]{1,0:T(8,128)S(1)}, f32[8,128]{1,0:T(8,128)S(1)}, u32[]{:S(2)}, u32[]{:S(2)}) collective-permute-start(f32[8,128]{1,0:T(8,128)S(1)} %get-tuple-element.24), channel_id=1, source_target_pairs={{0,1},{1,0},{2,3},{3,2},{4,5},{5,4},{6,7},{7,6},{8,9},{9,8},{10,11... | collective-permute-start | bytes 12296 | tf_op jit(solution)/shard_map/ppermute | solution.py:402
  20.3 3.0 %collective-permute-start.3 = (f32[8,128]{1,0:T(8,128)S(1)}, f32[8,128]{1,0:T(8,128)S(1)}, u32[]{:S(2)}, u32[]{:S(2)}) collective-permute-start(f32[8,128]{1,0:T(8,128)S(1)} %max.12), channel_id=1, source_target_pairs={{0,3},{1,2},{2,1},{3,0},{4,7},{5,6},{6,5},{7,4},{8,11},{9,10},{10,... | collective-permute-start | bytes 12296 | tf_op jit(solution)/shard_map/ppermute | solution.py:402
  23.3 3.0 %collective-permute-start.4 = (f32[8,128]{1,0:T(8,128)S(1)}, f32[8,128]{1,0:T(8,128)S(1)}, u32[]{:S(2)}, u32[]{:S(2)}) collective-permute-start(f32[8,128]{1,0:T(8,128)S(1)} %max.13), channel_id=1, source_target_pairs={{0,5},{1,4},{2,7},{3,6},{4,1},{5,0},{6,3},{7,2},{8,13},{9,12},{10,... | collective-permute-start | bytes 12296 | tf_op jit(solution)/shard_map/ppermute | solution.py:402
  26.3 4.1 %collective-permute-start.5 = (f32[8,128]{1,0:T(8,128)S(1)}, f32[8,128]{1,0:T(8,128)S(1)}, u32[]{:S(2)}, u32[]{:S(2)}) collective-permute-start(f32[8,128]{1,0:T(8,128)S(1)} %max.14), channel_id=1, source_target_pairs={{0,9},{1,8},{2,11},{3,10},{4,13},{5,12},{6,15},{7,14},{8,1},{9,0},... | collective-permute-start | bytes 12296 | tf_op jit(solution)/shard_map/ppermute | solution.py:402
